TPU v7x, 128 devices: a whole 4x4x4 slice. The times are simulated.
128 devices in a mesh: pre: 8 (over x, core), row: 16 (over z, y).
Axes of the slice: x: 4, y: 4, z: 4, core: 2. Of those that a mesh axis runs over, the one named last changes fastest.
Arguments:
- queries: bfloat16 [1024, 12288], P(('pre', 'row')), may hold values from -9 to 9
- prompt_ids: int32 [1024, 1], P(('pre', 'row')), may hold values from 0 to 7; in each aligned block of 8 rows (0 to 7, 8 to 15, ...) at most 2 rows name the same one
- suffix_len: int32 [1024], P(('pre', 'row')), may hold values from 1 to 256, as said below
- page_table: int32 [1024, 16], P(('pre', 'row')), may hold values from 0 to 127, as said below
- suffix_pool: bfloat16 [16384, 16, 2048], P(('pre', 'row')), may hold values from -24 to 24
- prefix_kv: bfloat16 [8, 16384, 2048], P('pre', 'row'), may hold values from -18 to 18
Outputs:
- attention: bfloat16 [1024, 12288], P(('pre', 'row'))
Inputs may be any that keep to these rules, and one draw needn't show every extreme that they name: `suffix_len`: each device's 8 rows include one of length 256. `page_table`: the rows of one device name each of that device's 128 pages exactly once. `prompt_ids`: in the rows of one device no prompt is named by more than 2 rows.
All inputs are finite; a program needn't handle non-finite values.
Results may differ from a plain program's by a relative error of at most 0.014.
Values may be sent and summed in bfloat16 or wider, within the bound.
No kernel may reach another device: no remote copies, remote signals or barrier semaphores. Data moves between devices by JAX's collectives and lax.ppermute only.
A program may use at most 512 MiB of HBM per device.

v0:
```python
import math

import jax
import jax.numpy as jnp
from jax import lax
from jax.sharding import PartitionSpec as P

KVH = 8
HD = 128
CAP = 2


def combined_all(array, axis, combine):
    everything = jax.tree.map(lambda part: lax.all_gather(part, axis), array)
    initial = jax.tree.map(lambda part: part[0], everything)

    def lap(k, so_far):
        return combine(so_far, jax.tree.map(lambda part: part[k], everything))

    return lax.fori_loop(1, lax.axis_size(axis), lap, initial)


def combine_parts(former, latter):
    highest = jnp.maximum(former[0], latter[0])
    left_scale = jnp.exp(former[0] - highest)
    right_scale = jnp.exp(latter[0] - highest)
    return (
        highest,
        former[1] * left_scale + latter[1] * right_scale,
        former[2] * left_scale[..., None] + latter[2] * right_scale[..., None],
    )


def body(queries, prompt_ids, suffix_len, page_table, suffix_pool, prefix_kv):
    owners = lax.axis_size("pre")
    row_count = queries.shape[0]
    kv_width = KVH * HD
    group_size = queries.shape[1] // kv_width
    slot_count = owners * CAP
    score_scale = 1.0 / math.sqrt(HD)
    prompt_of = prompt_ids[:, 0]
    position = jnp.arange(row_count)
    earlier = (prompt_of[:, None] == prompt_of[None, :]) & (position[None, :] < position[:, None])
    rank_within = jnp.sum(earlier.astype(jnp.int32), axis=1)
    slot_of = prompt_of * CAP + rank_within
    selector = slot_of[None, :] == jnp.arange(slot_count)[:, None]
    outgoing = jnp.dot(
        selector.astype(jnp.bfloat16), queries, preferred_element_type=jnp.float32
    ).astype(jnp.bfloat16)
    arrived = lax.all_to_all(
        outgoing.reshape(owners, CAP, -1), "pre", split_axis=0, concat_axis=0, tiled=True
    )
    gathered = lax.all_gather(arrived.reshape(slot_count, -1), "row", axis=0, tiled=True)
    total_slots = gathered.shape[0]
    prefix_rows = prefix_kv[0]

    def one_head(index):
        query_rows = lax.dynamic_slice_in_dim(gathered, index * group_size * HD, group_size * HD, 1)
        query_rows = query_rows.reshape(total_slots * group_size, HD)
        key_rows = lax.dynamic_slice_in_dim(prefix_rows, index * HD, HD, 1)
        value_rows = lax.dynamic_slice_in_dim(prefix_rows, kv_width + index * HD, HD, 1)
        scores = (
            jnp.einsum("qd,td->qt", query_rows, key_rows, preferred_element_type=jnp.float32)
            * score_scale
        )
        head_max = jnp.max(scores, axis=1)
        expo_terms = jnp.exp(scores - head_max[:, None])
        head_total = jnp.sum(expo_terms, axis=1)
        head_out = jnp.dot(
            expo_terms.astype(jnp.bfloat16), value_rows, preferred_element_type=jnp.float32
        )
        return (
            head_max.reshape(total_slots, group_size),
            head_total.reshape(total_slots, group_size),
            head_out.reshape(total_slots, group_size, HD),
        )

    maxima, totals, output = lax.map(one_head, jnp.arange(KVH, dtype=jnp.int32))
    own_start = lax.axis_index("row") * slot_count
    maxima, totals, output = combined_all((maxima, totals, output), "row", combine_parts)
    maxima = lax.dynamic_slice_in_dim(maxima, own_start, slot_count, 1)
    totals = lax.dynamic_slice_in_dim(totals, own_start, slot_count, 1)
    output = lax.dynamic_slice_in_dim(output, own_start, slot_count, 1)
    returned = (
        lax.all_to_all(
            output.reshape(KVH, owners, CAP, group_size, HD),
            "pre",
            split_axis=1,
            concat_axis=1,
            tiled=True,
        ),
        lax.all_to_all(
            totals.reshape(KVH, owners, CAP, group_size),
            "pre",
            split_axis=1,
            concat_axis=1,
            tiled=True,
        ),
        lax.all_to_all(
            maxima.reshape(KVH, owners, CAP, group_size),
            "pre",
            split_axis=1,
            concat_axis=1,
            tiled=True,
        ),
    )
    picker = selector.astype(jnp.float32)
    pre_output = jnp.einsum(
        "sr,ksgd->rkgd",
        picker,
        returned[0].reshape(KVH, slot_count, group_size, HD),
        precision=lax.Precision.HIGHEST,
    )
    pre_total = jnp.einsum(
        "sr,ksg->rkg",
        picker,
        returned[1].reshape(KVH, slot_count, group_size),
        precision=lax.Precision.HIGHEST,
    )
    pre_max = jnp.einsum(
        "sr,ksg->rkg",
        picker,
        returned[2].reshape(KVH, slot_count, group_size),
        precision=lax.Precision.HIGHEST,
    )
    suffix_rows = suffix_pool[page_table]
    flattened = suffix_rows.reshape(row_count, -1, 2 * kv_width)
    suffix_span = flattened.shape[1]
    local_query = queries.reshape(row_count, KVH, group_size, HD)
    suffix_keys = flattened[:, :, :kv_width].reshape(row_count, suffix_span, KVH, HD)
    suffix_values = flattened[:, :, kv_width:].reshape(row_count, suffix_span, KVH, HD)
    scores = (
        jnp.einsum("rkgd,rtkd->rkgt", local_query, suffix_keys, preferred_element_type=jnp.float32)
        * score_scale
    )
    in_range = (jnp.arange(suffix_span)[None, :] < suffix_len[:, None])[:, None, None, :]
    scores = jnp.where(in_range, scores, -1e30)
    suffix_max = jnp.max(scores, axis=3)
    expo_terms = jnp.where(in_range, jnp.exp(scores - suffix_max[..., None]), 0.0)
    suffix_total = jnp.sum(expo_terms, axis=3)
    suffix_output = jnp.einsum(
        "rkgt,rtkd->rkgd",
        expo_terms.astype(jnp.bfloat16),
        suffix_values,
        preferred_element_type=jnp.float32,
    )
    merged = combine_parts(
        (pre_max, pre_total, pre_output), (suffix_max, suffix_total, suffix_output)
    )
    result = merged[2] / merged[1][..., None]
    return result.reshape(row_count, KVH * group_size * HD).astype(jnp.bfloat16)


def solution(mesh):
    return jax.shard_map(
        body,
        mesh=mesh,
        in_specs=(
            P(("pre", "row"), None),
            P(("pre", "row"), None),
            P(("pre", "row")),
            P(("pre", "row"), None),
            P(("pre", "row"), None, None),
            P("pre", "row", None),
        ),
        out_specs=P(("pre", "row"), None),
        check_vma=False,
    )
```

profile of v0, /device:TPU:0, one launch (start us, length us, event | category | flops | bytes accessed | tf_op | source)
XLA Modules:
  0.0 2010.7 jit_solution(5154680177942655451)
XLA Ops:
  9.3 13.1 all_to_all.20
  23.5 62.0 %all-gather.8.cloned.1.call-done = bf16[256,12288]{1,0:T(8,128)(2,1)} async-done(((bf16[16,12288]{1,0:T(8,128)(2,1)}), bf16[256,12288]{1,0:T(8,128)(2,1)}) %all-gather.8.cloned.1.call-update) | async-done | bytes 6291472 | tf_op jit(solution)/shard_map/all_gather | solution.py:53
  85.5 252.8 %while.35 = (s32[]{:T(128)}, f32[8,256,12]{1,0,2:T(8,128)S(1)}, f32[8,256,12]{1,0,2:T(8,128)}, f32[8,256,12,128]{3,1,2,0:T(8,128)}, s32[8]{0:T(128)S(1)}, /*inde...) while((s32[]{:T(128)}, f32[8,256,12]{1,0,2:T(8,128)S(1)}, ...), condition=%wide.region_4.5_spmd, body=%wide.region_1.4_spmd.sunk | while | flops 1635772416 | bytes 50790720 | solution.py:78
  363.0 21.3 %all-gather.10.cloned.1.call-done = f32[128,256,12]{1,0,2:T(8,128)} async-done(((f32[8,256,12]{1,0,2:T(8,128)}), f32[128,256,12]{1,0,2:T(8,128)}) %all-gather.10.cloned.1.call-update) | async-done | bytes 1572880 | tf_op jit(solution)/shard_map/all_gather | solution.py:14
  385.1 46.0 %all-gather.12.cloned.1.call-done = f32[128,256,12]{1,0,2:T(8,128)} async-done(((f32[8,256,12]{1,0,2:T(8,128)}), f32[128,256,12]{1,0,2:T(8,128)}) %all-gather.12.cloned.1.call-update) | async-done | bytes 1572880 | tf_op jit(solution)/shard_map/all_gather | solution.py:14
  432.1 1053.2 %all-gather.14.cloned.1.call-done = f32[128,256,12,128]{3,1,2,0:T(8,128)} async-done(((f32[8,256,12,128]{3,1,2,0:T(8,128)}), f32[128,256,12,128]{3,1,2,0:T(8,128)}) %all-gather.14.cloned.1.call-update) | async-done | bytes 201326608 | tf_op jit(solution)/shard_map/all_gather | solution.py:14
  1495.9 17.6 copy.89
  1513.5 428.0 %while.36 = (s32[]{:T(128)}, f32[8,256,12]{1,0,2:T(8,128)S(1)}, f32[8,256,12]{1,0,2:T(8,128)S(1)}, f32[8,256,12,128]{3,2,1,0:T(8,128)}, f32[16,8,256,12]{2,1,0,3...) while((s32[]{:T(128)}, f32[8,256,12]{1,0,2:T(8,128)S(1)}, ...), condition=%wide.region_6.7_spmd, body=%wide.region_5.6_spmd.sunk | while | flops 9584645 | bytes 64290968 | solution.py:20
  1526.1 16.1 fusion.67
  1554.6 16.1 fusion.67
  1583.1 16.1 fusion.67
  1611.6 16.1 fusion.67
  1640.2 16.1 fusion.67
  1668.7 16.1 fusion.67
  1685.8 10.6 constant_dynamic-slice_fusion.8
  1697.2 16.1 fusion.67
  1714.3 10.6 constant_dynamic-slice_fusion.8
  1725.7 16.1 fusion.67
  1742.9 10.6 constant_dynamic-slice_fusion.8
  1754.3 16.1 fusion.67
  1771.4 10.6 constant_dynamic-slice_fusion.8
  1782.8 16.1 fusion.67
  1799.9 10.6 constant_dynamic-slice_fusion.8
  1811.3 16.1 fusion.67
  1828.4 10.6 constant_dynamic-slice_fusion.8
  1839.8 16.1 fusion.67
  1857.0 10.6 constant_dynamic-slice_fusion.8
  1868.3 16.1 fusion.67
  1885.5 10.6 constant_dynamic-slice_fusion.8
  1896.9 16.1 fusion.67
  1925.4 16.1 fusion.67
  1956.8 17.6 copy.93
  (233 shorter events, 428.9 us)
Async XLA Ops:
  6.5 2.2 copy-start
  6.5 78.9 %all-gather.8.cloned.1.call-start = ((), (), s32[]{:S(2)}) async-start(), calls=%async_computation.4 | async-start | bytes 6684672 | tf_op jit(solution)/shard_map/all_gather | solution.py:53
  8.1 0.6 copy-start.2
  23.4 360.8 %all-gather.10.cloned.1.call-start = ((), (), s32[]{:S(2)}) async-start(), calls=%async_computation.5 | async-start | bytes 1671168 | tf_op jit(solution)/shard_map/all_gather | solution.py:14
  338.3 0.6 copy-start.1
  338.3 2.0 copy-start.4
  339.0 92.2 %all-gather.12.cloned.1.call-start = ((), (), s32[]{:S(2)}) async-start(), calls=%async_computation.6 | async-start | bytes 1671168 | tf_op jit(solution)/shard_map/all_gather | solution.py:14
  339.7 1145.5 %all-gather.14.cloned.1.call-start = ((), (), s32[]{:S(2)}) async-start(), calls=%async_computation.7 | async-start | bytes 213909504 | tf_op jit(solution)/shard_map/all_gather | solution.py:14
  350.5 12.4 copy-start.5
  1943.1 31.9 %all-to-all-start.2 = ((f32[8,1,192]{2,1,0:T(1,128)}), f32[8,1,192]{2,1,0:T(1,128)S(1)}, u32[]{:S(2)}, u32[]{:S(2)}) async-start(f32[8,1,192]{2,1,0:T(1,128)} %reshape.121), calls=%async_computation.2 | async-start | bytes 16384 | tf_op jit(solution)/shard_map/all_to_all | solution.py:99
  1956.8 38.2 %copy-start.3 = (s32[8]{0:T(128)S(1)}, s32[8]{0:T(128)}, u32[]{:S(2)}) copy-start(s32[8]{0:T(128)} %copy-done.2) | copy-start | bytes 100
  1975.0 10.3 all-to-all-start.3
  1985.4 16.6 all-to-all-start.1
Sparse Core Ops, SparseCore 0:
  23.5 61.9 all-gather.7
  339.1 45.1 all-gather.9
  386.4 44.7 all-gather.11
  433.1 1052.0 all-gather.13
where the time goes:
time: 2020 us; the launch traced here: 2010 us
  waiting for transfers between devices  1190 us (59%)
  local copies, waits for them, and re-layouts  332 us (16%)
  other arithmetic  313 us (15%)
  matrix products  121 us (6%)
    all_gather x3, waiting for transfers between devices, combined_all(): everything = jax.tree.map(lambda part: lax.all_gather(part, axis), array)  1120 us
    add x15, other arithmetic, combine_parts(): former[2] * left_scale[..., None] + latter[2] * right_scale[..., None]  241 us
    dynamic_slice x15, local copies, waits for them, and re-layouts, lap(): return combine(so_far, jax.tree.map(lambda part: part[k], everything))  160 us
    all_gather x1, waiting for transfers between devices, body(): lax.all_gather(arrived.reshape(slot_count, -1), 'row', axis=0, tiled=True)  62 us
    dot_general x8, matrix products, one_head(): jnp.einsum('qd,td->qt', query_rows, key_rows, preferred_element_type=jnp....  58.2 us
    dot_general x8, matrix products, one_head(): jnp.dot(expo_terms.astype(jnp.bfloat16), value_rows, preferred_element_ty...  54.4 us
    reduce_sum x8, other arithmetic, one_head(): head_total = jnp.sum(expo_terms, axis=1)  53.2 us
    dynamic_update_slice x40, local copies, waits for them, and re-layouts, body(): maxima, totals, output = lax.map(one_head, jnp.arange(KVH, dtype=jnp.int32))  40.7 us
  transfers between devices with their start and end apart: 7, of which 6 were waited for; matrix products, arithmetic and copies ran while one was open for 3% of the time, Pallas kernels for 0%

commit v1 on v0

v1 whole, which is shorter than its diff:
```python
import functools
import math

import jax
import jax.numpy as jnp
from jax import lax
from jax.experimental import pallas as pl
from jax.experimental.pallas import tpu as pltpu
from jax.sharding import PartitionSpec as P

KVH = 8
HD = 128
CAP = 2
GROUP = 12
ROWS = 8
WIDE = GROUP * HD
KVW = KVH * HD
NX, NC, NZ, NY = 4, 2, 4, 4
DEVS = NX * NC * NZ * NY
BLOCK = 1024
PAGE = 16
MAXP = 16
SPAN = PAGE * MAXP
SLOTS = 2 * CAP
ARR = DEVS * SLOTS
HALF = ARR // 2
TILE = 32
EMPTY = 256.0
SCALE = 1.0 / math.sqrt(HD)
AXES = ("pre", "row")
MB = 1 << 20
F32 = jnp.float32
BF16 = jnp.bfloat16


def dot(a, b):
    return jnp.dot(a, b, preferred_element_type=F32)


def dot_t(a, b):
    return lax.dot_general(a, b, (((1,), (1,)), ((), ())), preferred_element_type=F32)


def iota(shape, dim):
    return lax.broadcasted_iota(jnp.int32, shape, dim)


def device_number(x, c, z, y):
    return ((x * NC + c) * NZ + z) * NY + y


def routes(k, cross):
    pairs = []
    for x in range(NX):
        for c in range(NC):
            for z in range(NZ):
                for y in range(NY):
                    if (c ^ cross) == 0:
                        to = device_number(x, 0, (z + k) % NZ, y)
                    else:
                        to = device_number(x, 1, z, (y + k) % NY)
                    pairs.append((device_number(x, c, z, y), to))
    return pairs


def split_heads_kernel(head_ref, kv_ref, *refs):
    outs, sems = refs[:-1], refs[-1]
    copies = []
    for i, out in enumerate(outs):
        for part in range(2):
            start = pl.multiple_of(part * KVW + head_ref[i] * HD, HD)
            copies.append(
                pltpu.make_async_copy(
                    kv_ref.at[0, :, pl.ds(start, HD)], out.at[part], sems.at[i, part]
                )
            )
    for copy in copies:
        copy.start()
    for copy in copies:
        copy.wait()


def split_heads(heads, prefix_kv):
    n = heads.shape[0]
    return pl.pallas_call(
        split_heads_kernel,
        out_shape=[jax.ShapeDtypeStruct((2, BLOCK, HD), BF16)] * n,
        in_specs=[pl.BlockSpec(memory_space=pltpu.SMEM), pl.BlockSpec(memory_space=pl.ANY)],
        out_specs=[pl.BlockSpec(memory_space=pl.ANY)] * n,
        scratch_shapes=[pltpu.SemaphoreType.DMA((n, 2))],
        name="split_heads",
    )(heads, prefix_kv)


def send_kernel(col_ref, row_ref, q_ref, out_ref):
    wide = NY * ROWS
    mates = (col_ref[...] == row_ref[...]) & (
        iota((ROWS, wide), 0) < iota((ROWS, wide), 1) % ROWS
    )
    rank = jnp.sum(mates.astype(jnp.int32), axis=0, keepdims=True)
    slot = row_ref[...] * CAP + rank
    rows = NX * NY * SLOTS
    r = iota((rows, wide), 0)
    base = r // (NY * SLOTS) * SLOTS
    lane = iota((rows, wide), 1)
    first = (base + r % SLOTS == slot) & (lane < ROWS)
    second = (base + (r + CAP) % SLOTS == slot) & (r // SLOTS % NY == lane // ROWS)
    first = first.astype(F32)
    second = second.astype(F32)
    empty_first = (1.0 - jnp.sum(first, axis=1, keepdims=True)) * EMPTY
    empty_second = (1.0 - jnp.sum(second, axis=1, keepdims=True)) * EMPTY
    first = first[:, :ROWS].astype(BF16)
    second = second.astype(BF16)
    unit = NY * SLOTS
    for z in range(NZ):
        piece = dot(first, q_ref[:, z * WIDE : (z + 1) * WIDE]) + empty_first
        piece = piece.astype(BF16)
        for x in range(NX):
            at = device_number(x, 0, z, 0) * SLOTS
            out_ref[at : at + unit, :] = piece[x * unit : (x + 1) * unit]
    stacked = jnp.concatenate(
        [
            q_ref[:, (NZ + y) * WIDE : (NZ + y + 1) * WIDE].astype(F32)
            for y in range(NY)
        ],
        axis=0,
    ).astype(BF16)
    piece = (dot(second, stacked) + empty_second).astype(BF16)
    for x in range(NX):
        for z in range(NZ):
            at = device_number(x, 1, z, 0) * SLOTS
            out_ref[at : at + unit, :] = piece[x * unit : (x + 1) * unit]


def fill_sends(prompt_ids, queries):
    return pl.pallas_call(
        send_kernel,
        out_shape=jax.ShapeDtypeStruct((ARR, WIDE), BF16),
        compiler_params=pltpu.CompilerParams(vmem_limit_bytes=32 * MB),
        name="fill_sends",
    )(prompt_ids, jnp.tile(prompt_ids.reshape(1, ROWS), (1, NY)), queries)


def suffix_kernel(table_ref, len_ref, q_ref, pool_ref, out_ref, lse_ref, kv, sems):
    i = pl.program_id(0)

    def fetch(row, slot):
        for p in range(MAXP):
            pltpu.make_async_copy(
                pool_ref.at[table_ref[row, p]],
                kv.at[slot, pl.ds(p * PAGE, PAGE), :],
                sems.at[slot],
            ).start()

    @pl.when(i == 0)
    def _():
        fetch(0, 0)

    @pl.when(i + 1 < ROWS)
    def _():
        fetch(i + 1, (i + 1) % 2)

    slot = i % 2
    pltpu.make_async_copy(kv.at[slot], kv.at[slot], sems.at[slot]).wait()
    in_range = iota((16, SPAN), 1) < len_ref[i]
    for h in range(KVH):
        keys = kv[slot, :, h * HD : (h + 1) * HD]
        values = kv[slot, :, KVW + h * HD : KVW + (h + 1) * HD]
        scores = jnp.where(in_range, dot_t(q_ref[0, h], keys) * SCALE, -1e30)
        top = jnp.max(scores, axis=1, keepdims=True)
        weights = jnp.where(in_range, jnp.exp(scores - top), 0.0)
        total = jnp.sum(weights, axis=1, keepdims=True)
        out_ref[0, h] = dot(weights.astype(BF16), values) / total
        lse_ref[0, h] = jnp.broadcast_to(top + jnp.log(total), (16, HD))


def suffix(page_table, suffix_len, queries, suffix_pool):
    q = queries.reshape(ROWS, KVH, GROUP, HD)
    q = jnp.pad(q, ((0, 0), (0, 0), (0, 16 - GROUP), (0, 0)))
    spec = pl.BlockSpec((1, KVH, 16, HD), lambda i: (i, 0, 0, 0))
    smem = pl.BlockSpec(memory_space=pltpu.SMEM)
    shape = jax.ShapeDtypeStruct((ROWS, KVH, 16, HD), F32)
    out, lse = pl.pallas_call(
        suffix_kernel,
        grid=(ROWS,),
        out_shape=[shape, shape],
        in_specs=[smem, smem, spec, pl.BlockSpec(memory_space=pl.ANY)],
        out_specs=[spec, spec],
        scratch_shapes=[pltpu.VMEM((2, SPAN, 2 * KVW), BF16), pltpu.SemaphoreType.DMA((2,))],
        compiler_params=pltpu.CompilerParams(vmem_limit_bytes=32 * MB),
        cost_estimate=pl.CostEstimate(
            flops=4 * ROWS * KVH * 256 * SPAN * HD, bytes_accessed=9 * MB, transcendentals=0
        ),
        name="suffix",
    )(page_table, suffix_len, q, suffix_pool)
    return (
        out[:, :, :GROUP].reshape(ROWS, KVH * WIDE),
        lse[:, :, :GROUP].reshape(ROWS, KVH * WIDE),
    )


def prefix_kernel(x_ref, *refs):
    kv_refs = refs[:8]
    out_ref, qs, os, ls = refs[8:]
    log2e = 1.0 / math.log(2.0)
    pick = (iota((8, HD), 1) == 0).astype(BF16)
    mark_row = dot_t(pick, x_ref[:, :HD])
    held_row = mark_row < EMPTY / 2
    turn_row = iota((8, ARR), 1) % SLOTS // CAP
    before = (iota((ARR, ARR), 0) <= iota((ARR, ARR), 1)) & (
        iota((ARR, ARR), 0) % SLOTS // CAP == iota((ARR, ARR), 1) % SLOTS // CAP
    )
    place_row = dot(held_row.astype(BF16), before.astype(BF16)).astype(jnp.int32) - 1
    held_col = x_ref[:, :HD].astype(F32)[:, 0:1] < EMPTY / 2
    upto = (iota((ARR, ARR), 1) <= iota((ARR, ARR), 0)) & (
        iota((ARR, ARR), 0) % SLOTS // CAP == iota((ARR, ARR), 1) % SLOTS // CAP
    )
    held_wide = jnp.broadcast_to(held_col.astype(F32), (ARR, HD)).astype(BF16)
    place_col = dot(upto.astype(BF16), held_wide)[:, 0:1].astype(jnp.int32) - 1
    turn_col = iota((ARR, 1), 0) % SLOTS // CAP

    for turn in range(2):
        chosen_row = held_row & (turn_row == turn)
        gather = (
            (place_row[0:1] == iota((HALF, ARR), 0)) & chosen_row[0:1]
        ).astype(BF16)
        for g in range(GROUP):
            qs[turn, g] = dot(gather, x_ref[:, g * HD : (g + 1) * HD]).astype(BF16)
        os[turn] = jnp.zeros((GROUP, HALF, HD), BF16)
        ls[turn] = jnp.zeros((HALF, HD), BF16)
        count = jnp.sum(chosen_row[0:1].astype(jnp.int32))

        def tile(t, carry, turn=turn):
            at = pl.multiple_of(t * TILE, TILE)
            q = qs[turn, :, pl.ds(at, TILE), :].reshape(GROUP * TILE, HD)
            top = total = acc = None
            for k in range(4):
                kv = kv_refs[k * 2 + turn]
                s = dot_t(q, kv[0])
                high = jnp.max(s, axis=1, keepdims=True)
                if k > 0:
                    high = jnp.maximum(top, high)
                p = jnp.exp2(s * (SCALE * log2e) - high * (SCALE * log2e))
                part_total = jnp.sum(p, axis=1, keepdims=True)
                part = dot(p.astype(BF16), kv[1])
                if k > 0:
                    fade = jnp.exp2((top - high) * (SCALE * log2e))
                    total = total * fade + part_total
                    acc = acc * fade + part
                else:
                    total, acc = part_total, part
                top = high
            os[turn, :, pl.ds(at, TILE), :] = (
                (acc / total).astype(BF16).reshape(GROUP, TILE, HD)
            )
            lse = (top * SCALE + jnp.log(total)).reshape(GROUP, TILE, 1)
            lane = iota((TILE, HD), 1)
            wide = jnp.zeros((TILE, HD), F32)
            for g in range(GROUP):
                mine = (lane == g) | (lane == g + GROUP) | (lane == g + 2 * GROUP)
                wide = wide + jnp.where(mine, lse[g], 0.0)
            one = wide.astype(BF16).astype(F32)
            two = (wide - one).astype(BF16).astype(F32)
            three = wide - one - two
            split = jnp.where(lane < GROUP, one, jnp.where(lane < 2 * GROUP, two, three))
            ls[turn, pl.ds(at, TILE), :] = split.astype(BF16)
            return carry

        lax.fori_loop(0, (count + TILE - 1) // TILE, tile, 0)

    scatter = [
        ((place_col == iota((ARR, HALF), 1)) & held_col & (turn_col == turn)).astype(BF16)
        for turn in range(2)
    ]
    for g in range(GROUP):
        piece = dot(scatter[0], os[0, g]) + dot(scatter[1], os[1, g])
        out_ref[:, g * HD : (g + 1) * HD] = piece.astype(BF16)
    piece = dot(scatter[0], ls[0]) + dot(scatter[1], ls[1])
    out_ref[:, WIDE:] = piece.astype(BF16)


def prefix(arrived, kv):
    return pl.pallas_call(
        prefix_kernel,
        out_shape=jax.ShapeDtypeStruct((ARR, WIDE + HD), BF16),
        scratch_shapes=[
            pltpu.VMEM((2, GROUP, HALF, HD), BF16),
            pltpu.VMEM((2, GROUP, HALF, HD), BF16),
            pltpu.VMEM((2, HALF, HD), BF16),
        ],
        compiler_params=pltpu.CompilerParams(vmem_limit_bytes=56 * MB),
        cost_estimate=pl.CostEstimate(
            flops=20 * 10**9, bytes_accessed=8 * MB, transcendentals=0
        ),
        name="prefix",
    )(arrived, *kv)


def merge_kernel(at_ref, back_ref, so_ref, sl_ref, out_ref):
    sel = (at_ref[...] == iota((KVH * 4 * ROWS, ARR), 1)).astype(BF16)
    mine = dot(sel, back_ref[...])
    spread = (
        (iota((HD, WIDE), 0) % GROUP == iota((HD, WIDE), 1) // HD)
        & (iota((HD, WIDE), 0) < 3 * GROUP)
    ).astype(BF16)
    lse = dot(mine[:, WIDE:].astype(BF16), spread)
    for h in range(KVH):
        cut = slice(h * WIDE, (h + 1) * WIDE)
        rows = [slice((h * 4 + j) * ROWS, (h * 4 + j + 1) * ROWS) for j in range(4)]
        parts = [(lse[r], mine[r, :WIDE]) for r in rows]
        parts.append((sl_ref[:, cut], so_ref[:, cut]))
        top = functools.reduce(jnp.maximum, [p[0] for p in parts])
        weights = [jnp.exp(p[0] - top) for p in parts]
        total = functools.reduce(jnp.add, weights)
        acc = functools.reduce(jnp.add, [w * p[1] for w, p in zip(weights, parts)])
        out_ref[:, cut] = (acc / total).astype(BF16)


def merge(prompt_ids, back, so, sl):
    prompt = prompt_ids[:, 0]
    earlier = jnp.arange(ROWS)[None, :] < jnp.arange(ROWS)[:, None]
    rank = jnp.sum(((prompt[:, None] == prompt[None, :]) & earlier).astype(jnp.int32), axis=1)
    h = jnp.arange(KVH)[:, None, None]
    j = jnp.arange(4)[None, :, None]
    c = h // 4
    z = jnp.where(c == 0, h, j)
    y = jnp.where(c == 0, j, h - 4)
    place = (prompt % 2 != c).astype(jnp.int32) * CAP + rank
    at = device_number(prompt // 2, c, z, y) * SLOTS + place
    return pl.pallas_call(
        merge_kernel,
        out_shape=jax.ShapeDtypeStruct((ROWS, KVH * WIDE), BF16),
        compiler_params=pltpu.CompilerParams(vmem_limit_bytes=32 * MB),
        name="merge",
    )(at.reshape(-1, 1), back, so, sl)


def exchange(array):
    width = array.shape[1]
    moved = lax.all_to_all(
        array.reshape(DEVS, SLOTS, width), AXES, split_axis=0, concat_axis=0, tiled=True
    )
    return moved.reshape(ARR, width)


def body(queries, prompt_ids, suffix_len, page_table, suffix_pool, prefix_kv):
    c = lax.axis_index("pre") % NC
    z = lax.axis_index("row") // NY
    y = lax.axis_index("row") % NY
    heads = jnp.stack(
        [
            jnp.where(c ^ cross == 0, (z + k) % NZ, NZ + (y + k) % NY)
            for k in range(4)
            for cross in range(2)
        ]
    ).astype(jnp.int32)
    pieces = split_heads(heads, prefix_kv)
    kv = [
        piece if n == 0 else lax.ppermute(piece, AXES, routes(n // 2, n % 2))
        for n, piece in enumerate(pieces)
    ]
    arrived = exchange(fill_sends(prompt_ids, queries))
    so, sl = suffix(page_table, suffix_len, queries, suffix_pool)
    back = exchange(prefix(arrived, kv))
    return merge(prompt_ids, back, so, sl)


def solution(mesh):
    return jax.shard_map(
        body,
        mesh=mesh,
        in_specs=(
            P(("pre", "row"), None),
            P(("pre", "row"), None),
            P(("pre", "row")),
            P(("pre", "row"), None),
            P(("pre", "row"), None, None),
            P("pre", "row", None),
        ),
        out_specs=P(("pre", "row"), None),
        check_vma=False,
    )
```

time: 2020 us -> 266 us (0.13)
  waiting for transfers between devices: 1190 us -> 22.1 us
  local copies, waits for them, and re-layouts: 332 us -> 16.5 us
  other arithmetic: 313 us -> 0.43 us
  Pallas kernels: 0 us -> 189 us
  matrix products: 121 us -> 0 us
  starting transfers between devices: 13.4 us -> 37.6 us
    all_gather x4 -> x0, waiting for transfers between devices: 1180 us -> none  [the longest x3 1120 us: combined_all(): everything = jax.tree.map(lambda part: lax.all_gather(part, axis), array)]
    add x31 -> x1, other arithmetic: 257 us -> 0.08 us  [merge(): at = device_number(prompt // 2, c, z, y) * SLOTS + place]
    pallas_call x0 -> x5, Pallas kernels: none -> 189 us  [the longest x1 129 us: split_heads(): pl.pallas_call(split_heads_kernel, out_shape=[jax.ShapeDtypeStruct((2, BL...]
    dynamic_slice x33 -> x0, local copies, waits for them, and re-layouts: 177 us -> none  [the longest x15 160 us: lap(): return combine(so_far, jax.tree.map(lambda part: part[k], everything))]
    dot_general x22 -> x0, matrix products: 121 us -> none  [the longest x8 58.2 us: one_head(): jnp.einsum('qd,td->qt', query_rows, key_rows, preferred_element_type=jnp....]
    reduce_sum x10 -> x1, other arithmetic: 54.6 us -> 0.18 us  [merge(): jnp.sum(((prompt[:, None] == prompt[None, :]) & earlier).astype(jnp.int32...]
    dynamic_update_slice x40 -> x0, local copies, waits for them, and re-layouts: 40.7 us -> none  [body(): maxima, totals, output = lax.map(one_head, jnp.arange(KVH, dtype=jnp.int32))]
    while x4 -> x0, local copies, waits for them, and re-layouts: 36.1 us -> none  [combined_all(): return lax.fori_loop(1, lax.axis_size(axis), lap, initial)]
  transfers between devices with their start and end apart: 7 -> 9, of which waited for: 6 -> 4; matrix products, arithmetic and copies ran while one was open for 3% -> 1% of each run, Pallas kernels for 0% -> 59%
where the time goes in v1:
time: 266 us
  Pallas kernels  189 us (71%)
  starting transfers between devices  37.6 us (14%)
  waiting for transfers between devices  22.1 us (8%)
  local copies, waits for them, and re-layouts  16.5 us (6%)
    pallas_call x1, Pallas kernels, split_heads(): pl.pallas_call(split_heads_kernel, out_shape=[jax.ShapeDtypeStruct((2, BL...  129 us
    all_to_all x2, starting transfers between devices, exchange(): lax.all_to_all(array.reshape(DEVS, SLOTS, width), AXES, split_axis=0, con...  30.1 us
    pallas_call x1, Pallas kernels, prefix(): pl.pallas_call(prefix_kernel, out_shape=jax.ShapeDtypeStruct((ARR, WIDE +...  29.2 us
    pallas_call x1, Pallas kernels, suffix(): pl.pallas_call(suffix_kernel, grid=(ROWS,), out_shape=[shape, shape], in_...  28.2 us
    ppermute x7, waiting for transfers between devices, body(): lax.ppermute(piece, AXES, routes(n // 2, n % 2))  22.1 us
    ppermute x7, starting transfers between devices, body(): lax.ppermute(piece, AXES, routes(n // 2, n % 2))  7.52 us
    reshape x2, local copies, waits for them, and re-layouts, exchange(): array.reshape(DEVS, SLOTS, width)  5.35 us
  transfers between devices with their start and end apart: 9, of which 4 were waited for; matrix products, arithmetic and copies ran while one was open for 1% of the time, Pallas kernels for 59%

profile of v1, /device:TPU:0, one launch (start us, length us, event | category | flops | bytes accessed | tf_op | source)
XLA Modules:
  0.0 265.8 jit_solution(15848213553420126619)
XLA Ops:
  0.0 0.7 copy.10.col_ref
  0.7 0.7 tile.8
  1.4 0.1 tile.9.row_ref
  1.5 0.9 copy-done.1
  2.4 0.5 fill_sends.1
  2.9 1.4 reshape.327
  4.2 11.2 %all-to-all-start = ((bf16[128,4,1536]{2,1,0:T(4,128)(2,1)}), bf16[128,4,1536]{2,1,0:T(4,128)(2,1)S(1)}, u32[]{:S(2)}, u32[]{:S(2)}) async-start(bf16[128,4,1536]{2,1,0:T(4,128)(2,1)} %reshape.327), calls=%async_computation | async-start | bytes 3145728 | tf_op jit(solution)/shard_map/all_to_all | solution.py:340
  15.6 0.7 stack.35.head_ref
  16.2 129.0 %split_heads.1 = (bf16[2,1024,128]{2,1,0:T(8,128)(2,1)}, bf16[2,1024,128]{2,1,0:T(8,128)(2,1)}, bf16[2,1024,128]{2,1,0:T(8,128)(2,1)}, bf16[2,1024,128]{2,1,0:T(...) custom-call(s32[8]{0:T(128)} %stack.35.head_ref, ...), custom_call_target="tpu_custom_call" | custom-call | tf_op jit(solution)/shard_map/split_heads/pallas_call | solution.py:85
  145.2 0.1 collective-permute-start
  145.3 1.2 collective-permute-start.1
  146.5 1.0 collective-permute-start.2
  147.6 3.5 %collective-permute-start.3 = (bf16[2,1024,128]{2,1,0:T(8,128)(2,1)}, bf16[2,1024,128]{2,1,0:T(8,128)(2,1)}, u32[]{:S(2)}, u32[]{:S(2)}) collective-permute-start(bf16[2,1024,128]{2,1,0:T(8,128)(2,1)} %get-tuple-element.19), channel_id=1, source_target_pairs={{0,8},{1,9},{2,10},{3,11},{4,12},{5,13},{6,14},{7,15},{8,0},{9,1},... | collective-permute-start | bytes 1572872 | tf_op jit(solution)/shard_map/ppermute | solution.py:359
  151.0 0.2 collective-permute-start.4
  151.2 1.5 collective-permute-start.5
  152.8 8.3 %collective-permute-done.1.refs_2_ = bf16[2,1024,128]{2,1,0:T(8,128)(2,1)S(1)} collective-permute-done((bf16[2,1024,128]{2,1,0:T(8,128)(2,1)}, bf16[2,1024,128]{2,1,0:T(8,128)(2,1)S(1)}, u32[]{:S(2)}, u32[]{:S(2)}) %collective-permute-start.1) | collective-permute-done | bytes 524320 | tf_op jit(solution)/shard_map/ppermute | solution.py:359
  161.1 1.4 reshape.328.x_ref
  162.5 11.4 %collective-permute-done.3.refs_4_ = bf16[2,1024,128]{2,1,0:T(8,128)(2,1)} collective-permute-done((bf16[2,1024,128]{2,1,0:T(8,128)(2,1)}, bf16[2,1024,128]{2,1,0:T(8,128)(2,1)}, u32[]{:S(2)}, u32[]{:S(2)}) %collective-permute-start.3) | collective-permute-done | bytes 524320 | tf_op jit(solution)/shard_map/ppermute | solution.py:359
  173.8 2.2 collective-permute-done.5.refs_6_
  176.0 0.3 collective-permute-done.6.refs_7_
  176.3 29.2 %prefix.1 = bf16[512,1664]{1,0:T(8,128)(2,1)} custom-call(bf16[512,1536]{1,0:T(8,128)(2,1)} %reshape.328.x_ref, bf16[2,1024,128]{2,1,0:T(8,128)(2,1)} %get-tuple-element.15.refs_0_, bf16[2,1024,128]{2,1,0:T(8,128)(2,1)} %copy-done.6, bf16[2,1024,128]{2,1,0:T(8,128)(2,1)} %copy-done.7, bf16[2,1024,128]{2,1,0:T(8,128)(2,1)} %copy-done.8, ...), custom_call_target="tpu_custom_call" | custom-call | flops 20000000000 | bytes 8388608 | tf_op jit(solution)/shard_map/prefix/pallas_call | solution.py:283
  205.5 4.0 %reshape.329 = bf16[128,4,1664]{2,1,0:T(4,128)(2,1)} reshape(bf16[512,1664]{1,0:T(8,128)(2,1)} %prefix.1) | data formatting | bytes 3407872 | tf_op jit(solution)/shard_map/reshape | solution.py:341
  209.5 19.0 %all-to-all-start.1 = ((bf16[128,4,1664]{2,1,0:T(4,128)(2,1)}), bf16[128,4,1664]{2,1,0:T(4,128)(2,1)}, u32[]{:S(2)}, u32[]{:S(2)}) async-start(bf16[128,4,1664]{2,1,0:T(4,128)(2,1)} %reshape.329), calls=%async_computation.1 | async-start | bytes 3407872 | tf_op jit(solution)/shard_map/all_to_all | solution.py:340
  228.4 0.2 reshape.331
  228.7 0.2 convert_reduce_fusion
  228.8 0.1 iota_select_fusion.1
  229.0 0.1 multiply_add_fusion
  229.1 0.1 reshape.335.at_ref
  229.3 3.4 %copy-done = bf16[128,16,2048]{2,1,0:T(8,128)(2,1)S(1)} copy-done((bf16[128,16,2048]{2,1,0:T(8,128)(2,1)S(1)}, bf16[128,16,2048]{2,1,0:T(8,128)(2,1)}, u32[]{:S(2)}) %copy-start) | copy-done | bytes 8388632
  232.7 28.2 %suffix.1 = (f32[8,8,16,128]{3,2,1,0:T(8,128)S(1)}, f32[8,8,16,128]{3,2,1,0:T(8,128)S(1)}) custom-call(s32[8,16]{1,0:T(8,128)S(1)} %copy-done.3, s32[8]{0:T(128)S(1)} %copy-done.4, bf16[8,8,16,128]{3,2,1,0:T(8,128)(2,1)S(1)} %pad.4.q_ref, bf16[128,16,2048]{2,1,0:T(8,128)(2,1)S(1)} %copy-done), custom_call_target="tpu_custom_call" | custom-call | flops 2147483648 | bytes 9437184 | tf_op jit(solution)/shard_map/suffix/pallas_call | solution.py:183
  261.0 2.9 %reshape.330.back_ref = bf16[512,1664]{1,0:T(8,128)(2,1)S(1)} reshape(bf16[128,4,1664]{2,1,0:T(4,128)(2,1)} %all-to-all-done.1) | data formatting | bytes 3407872 | tf_op jit(solution)/shard_map/reshape | solution.py:343
  263.8 1.9 merge.1
  (30 shorter events, 0.3 us)
Async XLA Ops:
  1.5 0.9 copy-start.1
  4.2 156.8 %all-to-all-start = ((bf16[128,4,1536]{2,1,0:T(4,128)(2,1)}), bf16[128,4,1536]{2,1,0:T(4,128)(2,1)S(1)}, u32[]{:S(2)}, u32[]{:S(2)}) async-start(bf16[128,4,1536]{2,1,0:T(4,128)(2,1)} %reshape.327), calls=%async_computation | async-start | bytes 3145728 | tf_op jit(solution)/shard_map/all_to_all | solution.py:340
  145.2 6.0 %collective-permute-start = (bf16[2,1024,128]{2,1,0:T(8,128)(2,1)}, bf16[2,1024,128]{2,1,0:T(8,128)(2,1)S(1)}, u32[]{:S(2)}, u32[]{:S(2)}) collective-permute-start(bf16[2,1024,128]{2,1,0:T(8,128)(2,1)} %get-tuple-element.16), channel_id=1, source_target_pairs={{0,16},{1,17},{2,18},{3,19},{4,20},{5,21},{6,22},{7,23},{8,24},{9,... | collective-permute-start | bytes 1572872 | tf_op jit(solution)/shard_map/ppermute | solution.py:359
  145.3 15.8 %collective-permute-start.1 = (bf16[2,1024,128]{2,1,0:T(8,128)(2,1)}, bf16[2,1024,128]{2,1,0:T(8,128)(2,1)S(1)}, u32[]{:S(2)}, u32[]{:S(2)}) collective-permute-start(bf16[2,1024,128]{2,1,0:T(8,128)(2,1)} %get-tuple-element.17), channel_id=1, source_target_pairs={{0,4},{1,5},{2,6},{3,7},{4,8},{5,9},{6,10},{7,11},{8,12},{9,13},{1... | collective-permute-start | bytes 1572872 | tf_op jit(solution)/shard_map/ppermute | solution.py:359
  146.5 15.9 %collective-permute-start.2 = (bf16[2,1024,128]{2,1,0:T(8,128)(2,1)}, bf16[2,1024,128]{2,1,0:T(8,128)(2,1)S(1)}, u32[]{:S(2)}, u32[]{:S(2)}) collective-permute-start(bf16[2,1024,128]{2,1,0:T(8,128)(2,1)} %get-tuple-element.18), channel_id=1, source_target_pairs={{0,17},{1,18},{2,19},{3,16},{4,21},{5,22},{6,23},{7,20},{8,25},{9,... | collective-permute-start | bytes 1572872 | tf_op jit(solution)/shard_map/ppermute | solution.py:359
  147.6 26.3 %collective-permute-start.3 = (bf16[2,1024,128]{2,1,0:T(8,128)(2,1)}, bf16[2,1024,128]{2,1,0:T(8,128)(2,1)}, u32[]{:S(2)}, u32[]{:S(2)}) collective-permute-start(bf16[2,1024,128]{2,1,0:T(8,128)(2,1)} %get-tuple-element.19), channel_id=1, source_target_pairs={{0,8},{1,9},{2,10},{3,11},{4,12},{5,13},{6,14},{7,15},{8,0},{9,1},... | collective-permute-start | bytes 1572872 | tf_op jit(solution)/shard_map/ppermute | solution.py:359
  151.0 22.8 %collective-permute-start.4 = (bf16[2,1024,128]{2,1,0:T(8,128)(2,1)}, bf16[2,1024,128]{2,1,0:T(8,128)(2,1)}, u32[]{:S(2)}, u32[]{:S(2)}) collective-permute-start(bf16[2,1024,128]{2,1,0:T(8,128)(2,1)} %get-tuple-element.20), channel_id=1, source_target_pairs={{0,18},{1,19},{2,16},{3,17},{4,22},{5,23},{6,20},{7,21},{8,26},{9,... | collective-permute-start | bytes 1572872 | tf_op jit(solution)/shard_map/ppermute | solution.py:359
  151.2 25.0 %copy-start.6 = (bf16[2,1024,128]{2,1,0:T(8,128)(2,1)}, bf16[2,1024,128]{2,1,0:T(8,128)(2,1)S(1)}, u32[]{:S(2)}) copy-start(bf16[2,1024,128]{2,1,0:T(8,128)(2,1)S(1)} %collective-permute-done.refs_1_) | copy-start | bytes 1572868
  151.2 24.8 %collective-permute-start.5 = (bf16[2,1024,128]{2,1,0:T(8,128)(2,1)}, bf16[2,1024,128]{2,1,0:T(8,128)(2,1)}, u32[]{:S(2)}, u32[]{:S(2)}) collective-permute-start(bf16[2,1024,128]{2,1,0:T(8,128)(2,1)} %get-tuple-element.21), channel_id=1, source_target_pairs={{0,12},{1,13},{2,14},{3,15},{4,0},{5,1},{6,2},{7,3},{8,4},{9,5},{1... | collective-permute-start | bytes 1572872 | tf_op jit(solution)/shard_map/ppermute | solution.py:359
  161.1 15.2 %copy-start.7 = (bf16[2,1024,128]{2,1,0:T(8,128)(2,1)}, bf16[2,1024,128]{2,1,0:T(8,128)(2,1)S(1)}, u32[]{:S(2)}) copy-start(bf16[2,1024,128]{2,1,0:T(8,128)(2,1)S(1)} %collective-permute-done.1.refs_2_) | copy-start | bytes 1572868
  161.1 15.2 %collective-permute-start.6 = (bf16[2,1024,128]{2,1,0:T(8,128)(2,1)}, bf16[2,1024,128]{2,1,0:T(8,128)(2,1)}, u32[]{:S(2)}, u32[]{:S(2)}) collective-permute-start(bf16[2,1024,128]{2,1,0:T(8,128)(2,1)} %get-tuple-element.22), channel_id=1, source_target_pairs={{0,19},{1,16},{2,17},{3,18},{4,23},{5,20},{6,21},{7,22},{8,27},{9,... | collective-permute-start | bytes 1572872 | tf_op jit(solution)/shard_map/ppermute | solution.py:359
  162.5 13.8 %copy-start.8 = (bf16[2,1024,128]{2,1,0:T(8,128)(2,1)}, bf16[2,1024,128]{2,1,0:T(8,128)(2,1)S(1)}, u32[]{:S(2)}) copy-start(bf16[2,1024,128]{2,1,0:T(8,128)(2,1)S(1)} %collective-permute-done.2.refs_3_) | copy-start | bytes 1572868
  209.4 19.0 %copy-start.2 = (bf16[8,12288]{1,0:T(8,128)(2,1)S(1)}, bf16[8,12288]{1,0:T(8,128)(2,1)}, u32[]{:S(2)}) copy-start(bf16[8,12288]{1,0:T(8,128)(2,1)} %q_ref.1) | copy-start | bytes 589828
  209.4 19.2 %copy-start.5 = (s32[8,1]{0,1:T(1,128)S(1)}, s32[8,1]{0,1:T(1,128)}, u32[]{:S(2)}) copy-start(s32[8,1]{0,1:T(1,128)} %param.7) | copy-start | bytes 100
  209.4 19.8 %copy-start.3 = (s32[8,16]{1,0:T(8,128)S(1)}, s32[8,16]{1,0:T(8,128)}, u32[]{:S(2)}) copy-start(s32[8,16]{1,0:T(8,128)} %table_ref.1) | copy-start | bytes 1540
  209.4 19.8 %copy-start.4 = (s32[8]{0:T(128)S(1)}, s32[8]{0:T(128)}, u32[]{:S(2)}) copy-start(s32[8]{0:T(128)} %len_ref.1) | copy-start | bytes 100
  209.5 51.5 %all-to-all-start.1 = ((bf16[128,4,1664]{2,1,0:T(4,128)(2,1)}), bf16[128,4,1664]{2,1,0:T(4,128)(2,1)}, u32[]{:S(2)}, u32[]{:S(2)}) async-start(bf16[128,4,1664]{2,1,0:T(4,128)(2,1)} %reshape.329), calls=%async_computation.1 | async-start | bytes 3407872 | tf_op jit(solution)/shard_map/all_to_all | solution.py:340
  229.3 3.4 %copy-start = (bf16[128,16,2048]{2,1,0:T(8,128)(2,1)S(1)}, bf16[128,16,2048]{2,1,0:T(8,128)(2,1)}, u32[]{:S(2)}) copy-start(bf16[128,16,2048]{2,1,0:T(8,128)(2,1)} %pool_ref.1) | copy-start | bytes 25165828

commit v2 on v1

v2 whole, which is shorter than its diff:
```python
import functools
import math

import jax
import jax.numpy as jnp
from jax import lax
from jax.experimental import pallas as pl
from jax.experimental.pallas import tpu as pltpu
from jax.sharding import PartitionSpec as P

KVH = 8
HD = 128
CAP = 2
GROUP = 12
ROWS = 8
WIDE = GROUP * HD
KVW = KVH * HD
NX, NC, NZ, NY = 4, 2, 4, 4
DEVS = NX * NC * NZ * NY
BLOCK = 1024
PAGE = 16
MAXP = 16
SPAN = PAGE * MAXP
SLOTS = 2 * CAP
HALVES = 2
PER_HALF = GROUP // HALVES
PAIRS = PER_HALF // 2
PART = PER_HALF * HD
LINES = HALVES * SLOTS
ARR = DEVS * LINES
HALF = DEVS * CAP
TILE = 64
CHUNK = 512
STRIPS = 4
EMPTY = 256.0
SCALE = 1.0 / math.sqrt(HD)
FACTOR = SCALE / math.log(2.0)
LEAST = 1e-26
MOST = 1e30
AXES = ("pre", "row")
MB = 1 << 20
F32 = jnp.float32
BF16 = jnp.bfloat16


def dot(a, b):
    return jnp.dot(a, b, preferred_element_type=F32)


def dot_t(a, b):
    return lax.dot_general(a, b, (((1,), (1,)), ((), ())), preferred_element_type=F32)


def iota(shape, dim):
    return lax.broadcasted_iota(jnp.int32, shape, dim)


def device_number(x, c, z, y):
    return ((x * NC + c) * NZ + z) * NY + y


def routes(k, cross):
    pairs = []
    for x in range(NX):
        for c in range(NC):
            for z in range(NZ):
                for y in range(NY):
                    if (c ^ cross) == 0:
                        to = device_number(x, 0, (z + k) % NZ, y)
                    else:
                        to = device_number(x, 1, z, (y + k) % NY)
                    pairs.append((device_number(x, c, z, y), to))
    return pairs


def split_heads_kernel(head_ref, kv_ref, *refs):
    outs, (held, sems) = refs[:-2], refs[-2:]
    inward, outward = [], []
    for i, out in enumerate(outs):
        for part in range(2):
            start = pl.multiple_of(part * KVW + head_ref[i] * HD, HD)
            inward.append(
                pltpu.make_async_copy(
                    kv_ref.at[0, :, pl.ds(start, HD)], held.at[i, part], sems.at[0, i, part]
                )
            )
            outward.append(
                pltpu.make_async_copy(held.at[i, part], out.at[part], sems.at[1, i, part])
            )
    for copy in inward:
        copy.start()
    for copy, onward in zip(inward, outward):
        copy.wait()
        onward.start()
    for copy in outward:
        copy.wait()


def split_heads(heads, prefix_kv):
    n = heads.shape[0]
    return pl.pallas_call(
        split_heads_kernel,
        out_shape=[jax.ShapeDtypeStruct((2, BLOCK, HD), BF16)] * n,
        in_specs=[pl.BlockSpec(memory_space=pltpu.SMEM), pl.BlockSpec(memory_space=pl.ANY)],
        out_specs=[pl.BlockSpec(memory_space=pl.ANY)] * n,
        scratch_shapes=[
            pltpu.VMEM((n, 2, BLOCK, HD), BF16),
            pltpu.SemaphoreType.DMA((2, n, 2)),
        ],
        compiler_params=pltpu.CompilerParams(vmem_limit_bytes=16 * MB),
        name="split_heads",
    )(heads, prefix_kv)


def send_kernel(col_ref, row_ref, q_ref, out_ref):
    wide = HALVES * NY * ROWS
    mates = (col_ref[...] == row_ref[...]) & (
        iota((ROWS, wide), 0) < iota((ROWS, wide), 1) % ROWS
    )
    rank = jnp.sum(mates.astype(jnp.int32), axis=0, keepdims=True)
    slot = row_ref[...] * CAP + rank
    unit = NY * LINES
    rows = NX * unit
    r = iota((rows, wide), 0)
    lane = iota((rows, wide), 1)
    base = r // unit * SLOTS
    half_fits = r // SLOTS % HALVES == lane // ROWS % HALVES
    first = (base + r % SLOTS == slot) & half_fits & (lane < HALVES * ROWS)
    second = (
        (base + (r + CAP) % SLOTS == slot)
        & half_fits
        & (r // LINES % NY == lane // (HALVES * ROWS))
    )
    first = first.astype(F32)
    second = second.astype(F32)
    empty_first = (1.0 - jnp.sum(first, axis=1, keepdims=True)) * EMPTY
    empty_second = (1.0 - jnp.sum(second, axis=1, keepdims=True)) * EMPTY
    first = first[:, : HALVES * ROWS].astype(BF16)
    second = second.astype(BF16)

    def stacked(heads):
        return jnp.concatenate(
            [
                q_ref[:, h * WIDE + half * PART : h * WIDE + (half + 1) * PART].astype(F32)
                for h in heads
                for half in range(HALVES)
            ],
            axis=0,
        ).astype(BF16)

    for z in range(NZ):
        piece = (dot(first, stacked([z])) + empty_first).astype(BF16)
        for x in range(NX):
            at = device_number(x, 0, z, 0) * LINES
            out_ref[at : at + unit, :] = piece[x * unit : (x + 1) * unit]
    piece = dot(second, stacked([NZ + y for y in range(NY)])) + empty_second
    piece = piece.astype(BF16)
    for x in range(NX):
        for z in range(NZ):
            at = device_number(x, 1, z, 0) * LINES
            out_ref[at : at + unit, :] = piece[x * unit : (x + 1) * unit]


def fill_sends(prompt_ids, queries):
    return pl.pallas_call(
        send_kernel,
        out_shape=jax.ShapeDtypeStruct((ARR, PART), BF16),
        compiler_params=pltpu.CompilerParams(vmem_limit_bytes=32 * MB),
        name="fill_sends",
    )(prompt_ids, jnp.tile(prompt_ids.reshape(1, ROWS), (1, HALVES * NY)), queries)


def suffix_kernel(table_ref, len_ref, q_ref, pool_ref, out_ref, lse_ref, kv, sems):
    for row in range(ROWS):
        for p in range(MAXP):
            pltpu.make_async_copy(
                pool_ref.at[table_ref[row, p]],
                kv.at[row, pl.ds(p * PAGE, PAGE), :],
                sems.at[row],
            ).start()

    def one(row, carry):
        pltpu.make_async_copy(kv.at[row], kv.at[row], sems.at[row]).wait()
        scores = jnp.concatenate(
            [
                dot_t(q_ref[row, h], kv[row, :, h * HD : (h + 1) * HD])
                for h in range(KVH)
            ],
            axis=0,
        )
        in_range = iota((KVH * 16, SPAN), 1) < len_ref[row]
        scores = jnp.where(in_range, scores * SCALE, -1e30)
        top = jnp.max(scores, axis=1, keepdims=True)
        weights = jnp.where(in_range, jnp.exp(scores - top), 0.0)
        total = jnp.sum(weights, axis=1, keepdims=True)
        scale = 1.0 / total
        lse = top + jnp.log(total)
        weights = weights.astype(BF16)
        for h in range(KVH):
            cut = slice(h * 16, (h + 1) * 16)
            values = kv[row, :, KVW + h * HD : KVW + (h + 1) * HD]
            out_ref[row, h] = dot(weights[cut], values) * scale[cut]
            lse_ref[row, h] = jnp.broadcast_to(lse[cut], (16, HD))
        return carry

    lax.fori_loop(0, ROWS, one, 0)


def suffix(page_table, suffix_len, queries, suffix_pool):
    q = queries.reshape(ROWS, KVH, GROUP, HD)
    q = jnp.pad(q, ((0, 0), (0, 0), (0, 16 - GROUP), (0, 0)))
    smem = pl.BlockSpec(memory_space=pltpu.SMEM)
    vmem = pl.BlockSpec(memory_space=pltpu.VMEM)
    shape = jax.ShapeDtypeStruct((ROWS, KVH, 16, HD), F32)
    out, lse = pl.pallas_call(
        suffix_kernel,
        out_shape=[shape, shape],
        in_specs=[smem, smem, vmem, pl.BlockSpec(memory_space=pl.ANY)],
        out_specs=[vmem, vmem],
        scratch_shapes=[
            pltpu.VMEM((ROWS, SPAN, 2 * KVW), BF16),
            pltpu.SemaphoreType.DMA((ROWS,)),
        ],
        compiler_params=pltpu.CompilerParams(vmem_limit_bytes=48 * MB),
        cost_estimate=pl.CostEstimate(
            flops=10**9, bytes_accessed=9 * MB, transcendentals=0
        ),
        name="suffix",
    )(page_table, suffix_len, q, suffix_pool)
    return (
        out[:, :, :GROUP].reshape(ROWS, KVH * WIDE),
        lse[:, :, :GROUP].reshape(ROWS, KVH * WIDE),
    )


def line_turn(line):
    return line // CAP % 2


def line_half(line):
    return line // SLOTS % HALVES


def gather_kernel(x_ref, q_ref, place_ref):
    pick = (iota((8, HD), 1) == 0).astype(BF16)
    held = dot_t(pick, x_ref[:, :HD]) < EMPTY / 2
    a, b = iota((ARR, ARR), 0), iota((ARR, ARR), 1)
    before = (a <= b) & (((a ^ b) & (LINES - CAP)) == 0)
    place = dot(held.astype(BF16), before.astype(BF16)).astype(jnp.int32) - 1
    place = jnp.where(held, place, -1)
    place_ref[...] = place
    line = iota((1, ARR), 1)
    for turn in range(2):
        for half in range(HALVES):
            mine = (line_turn(line) == turn) & (line_half(line) == half)
            row = jnp.where(mine, place[0:1], -1)
            gather = (row == iota((HALF, ARR), 0)).astype(BF16)
            for p in range(PAIRS):
                two = dot(gather, x_ref[:, p * 2 * HD : (p + 1) * 2 * HD]).astype(BF16)
                q_ref[turn, half * PER_HALF + 2 * p] = two[:, :HD]
                q_ref[turn, half * PER_HALF + 2 * p + 1] = two[:, HD:]


def gather_rows(arrived):
    return pl.pallas_call(
        gather_kernel,
        out_shape=[
            jax.ShapeDtypeStruct((2, GROUP, HALF, HD), BF16),
            jax.ShapeDtypeStruct((8, ARR), jnp.int32),
        ],
        compiler_params=pltpu.CompilerParams(vmem_limit_bytes=24 * MB),
        name="gather_rows",
    )(arrived)


def prefix_kernel(q_ref, place_ref, *refs):
    kv_refs = refs[:8]
    out_ref, os, ls, ks, vs, sems = refs[8:]
    copies = []
    for n in range(8):
        rows = pl.ds(n // 2 * BLOCK, BLOCK)
        copies.append(
            pltpu.make_async_copy(kv_refs[n].at[0], ks.at[n % 2, rows], sems.at[n, 0])
        )
        copies.append(
            pltpu.make_async_copy(
                kv_refs[n].at[1], vs.at[n % 2, rows, pl.ds(0, HD)], sems.at[n, 1]
            )
        )
    for copy in copies:
        copy.start()
    vs[:, :, HD:] = jnp.ones((2, 4 * BLOCK, HD), BF16)
    for turn in range(2):
        os[turn] = jnp.zeros((GROUP // 2, HALF, 2 * HD), BF16)
        ls[turn] = jnp.zeros((HALF, HD), BF16)
    place = place_ref[...]
    line = iota((1, ARR), 1)
    counts = [
        jnp.max(jnp.where(line_turn(line) == turn, place[0:1], -1)) + 1 for turn in range(2)
    ]
    for copy in copies:
        copy.wait()
    high_rows = GROUP * TILE
    strip = high_rows // STRIPS

    def finish(turn, at, acc, shift):
        total = acc[:, HD : HD + 1]
        out = (acc[:, :HD] / total).astype(BF16).reshape(GROUP, TILE, HD)
        for g in range(GROUP):
            os[turn, g // 2, pl.ds(at, TILE), g % 2 * HD : (g % 2 + 1) * HD] = out[g]
        lse = (shift + jnp.log(total)).reshape(GROUP, TILE, 1)
        lane = iota((TILE, HD), 1)
        wide = jnp.zeros((TILE, HD), F32)
        for g in range(GROUP):
            mine = (lane == g) | (lane == g + GROUP) | (lane == g + 2 * GROUP)
            wide = wide + jnp.where(mine, lse[g], 0.0)
        one = wide.astype(BF16).astype(F32)
        two = (wide - one).astype(BF16).astype(F32)
        three = wide - one - two
        split = jnp.where(lane < GROUP, one, jnp.where(lane < 2 * GROUP, two, three))
        ls[turn, pl.ds(at, TILE), :] = split.astype(BF16)

    for turn in range(2):

        def tile(t, carry, turn=turn):
            at = pl.multiple_of(t * TILE, TILE)
            q = q_ref[turn, :, pl.ds(at, TILE), :].reshape(high_rows, HD)
            accs = []
            for i in range(STRIPS):
                part_q = q[i * strip : (i + 1) * strip]
                acc = None
                score = dot_t(part_q, ks[turn, :CHUNK, :])
                for j in range(4 * BLOCK // CHUNK):
                    after = None
                    if (j + 1) * CHUNK < 4 * BLOCK:
                        after = dot_t(part_q, ks[turn, (j + 1) * CHUNK : (j + 2) * CHUNK, :])
                    weights = jnp.exp2(score * FACTOR).astype(BF16)
                    part = dot(weights, vs[turn, j * CHUNK : (j + 1) * CHUNK, :])
                    acc = part if acc is None else acc + part
                    score = after
                accs.append(acc)
            acc = jnp.concatenate(accs, axis=0)
            finish(turn, at, acc, 0.0)
            total = acc[:, HD : HD + 1]
            plain = (jnp.min(total) > LEAST) & (jnp.max(total) < MOST)

            @pl.when(jnp.logical_not(plain))
            def _():
                top = acc = None
                for k in range(4):
                    rows = slice(k * BLOCK, (k + 1) * BLOCK)
                    score = dot_t(q, ks[turn, rows, :])
                    high = jnp.max(score, axis=1, keepdims=True)
                    if k > 0:
                        high = jnp.maximum(top, high)
                    weights = jnp.exp2(score * FACTOR - high * FACTOR).astype(BF16)
                    part = dot(weights, vs[turn, rows, :])
                    if k > 0:
                        part = acc * jnp.exp2((top - high) * FACTOR) + part
                    top, acc = high, part
                finish(turn, at, acc, top * SCALE)

            return carry

        lax.fori_loop(0, (counts[turn] + TILE - 1) // TILE, tile, 0)

    place_col = jnp.transpose(place.astype(F32))[:, 0:1].astype(jnp.int32)
    line = iota((ARR, 1), 0)
    scatter = jnp.concatenate(
        [
            (
                jnp.where((line_turn(line) == turn) & (line_half(line) == half), place_col, -1)
                == iota((ARR, HALF), 1)
            ).astype(BF16)
            for turn in range(2)
            for half in range(HALVES)
        ],
        axis=1,
    )
    for p in range(PAIRS):
        source = jnp.concatenate(
            [os[turn, half * PAIRS + p] for turn in range(2) for half in range(HALVES)], axis=0
        )
        out_ref[:, p * 2 * HD : (p + 1) * 2 * HD] = dot(scatter, source).astype(BF16)
    source = jnp.concatenate([ls[0], ls[0], ls[1], ls[1]], axis=0)
    out_ref[:, PART:] = dot(scatter, source).astype(BF16)


def prefix(arrived, kv):
    rows, place = gather_rows(arrived)
    return pl.pallas_call(
        prefix_kernel,
        out_shape=jax.ShapeDtypeStruct((ARR, PART + HD), BF16),
        in_specs=[pl.BlockSpec(memory_space=pltpu.VMEM)] * 2
        + [pl.BlockSpec(memory_space=pl.ANY)] * 8,
        scratch_shapes=[
            pltpu.VMEM((2, GROUP // 2, HALF, 2 * HD), BF16),
            pltpu.VMEM((2, HALF, HD), BF16),
            pltpu.VMEM((2, 4 * BLOCK, HD), BF16),
            pltpu.VMEM((2, 4 * BLOCK, 2 * HD), BF16),
            pltpu.SemaphoreType.DMA((8, 2)),
        ],
        compiler_params=pltpu.CompilerParams(vmem_limit_bytes=48 * MB),
        cost_estimate=pl.CostEstimate(
            flops=20 * 10**9, bytes_accessed=8 * MB, transcendentals=0
        ),
        name="prefix",
    )(rows, place, *kv)


def merge_kernel(at_ref, back_ref, so_ref, sl_ref, out_ref):
    picked = KVH * 4 * ROWS
    line = iota((picked, ARR), 1)
    first = dot((at_ref[...] == line).astype(BF16), back_ref[...])
    second = dot((at_ref[...] + SLOTS == line).astype(BF16), back_ref[:, :PART])
    spread = (
        (iota((HD, WIDE), 0) % GROUP == iota((HD, WIDE), 1) // HD)
        & (iota((HD, WIDE), 0) < 3 * GROUP)
    ).astype(BF16)
    lse = dot(first[:, PART:].astype(BF16), spread)
    for h in range(KVH):
        cut = slice(h * WIDE, (h + 1) * WIDE)
        rows = [slice((h * 4 + j) * ROWS, (h * 4 + j + 1) * ROWS) for j in range(4)]
        parts = [
            (lse[r], jnp.concatenate([first[r, :PART], second[r]], axis=1)) for r in rows
        ]
        parts.append((sl_ref[:, cut], so_ref[:, cut]))
        top = functools.reduce(jnp.maximum, [p[0] for p in parts])
        weights = [jnp.exp(p[0] - top) for p in parts]
        total = functools.reduce(jnp.add, weights)
        acc = functools.reduce(jnp.add, [w * p[1] for w, p in zip(weights, parts)])
        out_ref[:, cut] = (acc / total).astype(BF16)


def merge(prompt_ids, back, so, sl):
    prompt = prompt_ids[:, 0]
    earlier = jnp.arange(ROWS)[None, :] < jnp.arange(ROWS)[:, None]
    rank = jnp.sum(((prompt[:, None] == prompt[None, :]) & earlier).astype(jnp.int32), axis=1)
    h = jnp.arange(KVH)[:, None, None]
    j = jnp.arange(4)[None, :, None]
    c = h // 4
    z = jnp.where(c == 0, h, j)
    y = jnp.where(c == 0, j, h - 4)
    place = (prompt % 2 != c).astype(jnp.int32) * CAP + rank
    at = device_number(prompt // 2, c, z, y) * LINES + place
    return pl.pallas_call(
        merge_kernel,
        out_shape=jax.ShapeDtypeStruct((ROWS, KVH * WIDE), BF16),
        compiler_params=pltpu.CompilerParams(vmem_limit_bytes=32 * MB),
        name="merge",
    )(at.reshape(-1, 1), back, so, sl)


def exchange(array):
    width = array.shape[1]
    moved = lax.all_to_all(
        array.reshape(DEVS, LINES, width), AXES, split_axis=0, concat_axis=0, tiled=True
    )
    return moved.reshape(ARR, width)


def body(queries, prompt_ids, suffix_len, page_table, suffix_pool, prefix_kv):
    c = lax.axis_index("pre") % NC
    z = lax.axis_index("row") // NY
    y = lax.axis_index("row") % NY
    heads = jnp.stack(
        [
            jnp.where(c ^ cross == 0, (z + k) % NZ, NZ + (y + k) % NY)
            for k in range(4)
            for cross in range(2)
        ]
    ).astype(jnp.int32)
    pieces = split_heads(heads, prefix_kv)
    pieces, queries = lax.optimization_barrier((pieces, queries))

    def move(n, piece):
        return lax.ppermute(piece, AXES, routes(n // 2, n % 2))

    kv = list(pieces)
    for n in (2, 3, 6, 7, 4):
        kv[n] = move(n, pieces[n])
    arrived = exchange(fill_sends(prompt_ids, queries))
    kv[2], kv[3], late, last, queries = lax.optimization_barrier(
        (kv[2], kv[3], pieces[5], pieces[1], queries)
    )
    kv[5] = move(5, late)
    kv[1] = move(1, last)
    so, sl = suffix(page_table, suffix_len, queries, suffix_pool)
    arrived, so, sl = lax.optimization_barrier((arrived, so, sl))
    back = exchange(prefix(arrived, kv))
    return merge(prompt_ids, back, so, sl)


def solution(mesh):
    return jax.shard_map(
        body,
        mesh=mesh,
        in_specs=(
            P(("pre", "row"), None),
            P(("pre", "row"), None),
            P(("pre", "row")),
            P(("pre", "row"), None),
            P(("pre", "row"), None, None),
            P("pre", "row", None),
        ),
        out_specs=P(("pre", "row"), None),
        check_vma=False,
    )
```

time: 266 us -> 165 us (0.62)
  Pallas kernels: 189 us -> 56.5 us
  waiting for transfers between devices: 22.1 us -> 51.6 us
  starting transfers between devices: 37.6 us -> 49.4 us
  local copies, waits for them, and re-layouts: 16.5 us -> 6.57 us
    pallas_call x1, Pallas kernels: 129 us -> 3.54 us  [split_heads(): pl.pallas_call(split_heads_kernel, out_shape=[jax.ShapeDtypeStruct((2, BL...]
    all_to_all x2, waiting for transfers between devices: 0.01 us -> 26.5 us  [exchange(): lax.all_to_all(array.reshape(DEVS, LINES, width), AXES, split_axis=0, con...]
    reshape x4 -> x0, local copies, waits for them, and re-layouts: 9.57 us -> none  [the longest x2 5.35 us: exchange(): array.reshape(DEVS, SLOTS, width)]
    ppermute x7, starting transfers between devices: 7.52 us -> 15.1 us  [move(): return lax.ppermute(piece, AXES, routes(n // 2, n % 2))]
    pallas_call x3 -> x4, Pallas kernels: 57.8 us -> 50.8 us  [the longest x1 41 us: prefix(): pl.pallas_call(prefix_kernel, out_shape=jax.ShapeDtypeStruct((ARR, PART +...]
    all_to_all x2, starting transfers between devices: 30.1 us -> 34.3 us  [exchange(): lax.all_to_all(array.reshape(DEVS, LINES, width), AXES, split_axis=0, con...]
    ppermute x7, waiting for transfers between devices: 22.1 us -> 25.1 us  [move(): return lax.ppermute(piece, AXES, routes(n // 2, n % 2))]
    unnamed x19 -> x23, local copies, waits for them, and re-layouts: 5.06 us -> 5.97 us
  transfers between devices with their start and end apart: 9 -> 9, of which waited for: 4 -> 3; matrix products, arithmetic and copies ran while one was open for 1% -> 1% of each run, Pallas kernels for 59% -> 5%
where the time goes in v2:
time: 165 us
  Pallas kernels  56.5 us (34%)
  waiting for transfers between devices  51.6 us (31%)
  starting transfers between devices  49.4 us (30%)
  local copies, waits for them, and re-layouts  6.57 us (4%)
    pallas_call x1, Pallas kernels, prefix(): pl.pallas_call(prefix_kernel, out_shape=jax.ShapeDtypeStruct((ARR, PART +...  41 us
    all_to_all x2, starting transfers between devices, exchange(): lax.all_to_all(array.reshape(DEVS, LINES, width), AXES, split_axis=0, con...  34.3 us
    all_to_all x2, waiting for transfers between devices, exchange(): lax.all_to_all(array.reshape(DEVS, LINES, width), AXES, split_axis=0, con...  26.5 us
    ppermute x7, waiting for transfers between devices, move(): return lax.ppermute(piece, AXES, routes(n // 2, n % 2))  25.1 us
    ppermute x7, starting transfers between devices, move(): return lax.ppermute(piece, AXES, routes(n // 2, n % 2))  15.1 us
    unnamed x23, local copies, waits for them, and re-layouts  5.97 us
    pallas_call x1, Pallas kernels, suffix(): pl.pallas_call(suffix_kernel, out_shape=[shape, shape], in_specs=[smem, s...  5.6 us
    pallas_call x1, Pallas kernels, split_heads(): pl.pallas_call(split_heads_kernel, out_shape=[jax.ShapeDtypeStruct((2, BL...  3.54 us
  transfers between devices with their start and end apart: 9, of which 3 were waited for; matrix products, arithmetic and copies ran while one was open for 1% of the time, Pallas kernels for 5%

profile of v2, /device:TPU:0, one launch (start us, length us, event | category | flops | bytes accessed | tf_op | source)
XLA Modules:
  0.0 164.8 jit_solution(15632302548287234231)
XLA Ops:
  0.0 0.1 stack.35.head_ref
  0.1 2.2 %copy-done = bf16[1,1024,2048]{2,1,0:T(8,128)(2,1)S(1)} copy-done((bf16[1,1024,2048]{2,1,0:T(8,128)(2,1)S(1)}, bf16[1,1024,2048]{2,1,0:T(8,128)(2,1)}, u32[]{:S(2)}) %copy-start) | copy-done | bytes 4194328
  2.3 3.5 %split_heads.1 = (bf16[2,1024,128]{2,1,0:T(8,128)(2,1)S(1)}, bf16[2,1024,128]{2,1,0:T(8,128)(2,1)}, bf16[2,1024,128]{2,1,0:T(8,128)(2,1)S(1)}, bf16[2,1024,128]{...) custom-call(s32[8]{0:T(128)S(1)} %stack.35.head_ref, ...), custom_call_target="tpu_custom_call" | custom-call | tf_op jit(solution)/shard_map/split_heads/pallas_call | solution.py:101
  5.8 0.8 copy-done.4
  6.6 0.1 copy.8.col_ref
  6.7 0.1 tile.2.row_ref
  6.8 1.7 %fill_sends.1 = bf16[1024,768]{1,0:T(8,128)(2,1)} custom-call(s32[8,1]{1,0:T(8,128)S(1)} %copy.8.col_ref, s32[1,64]{1,0:T(1,128)S(1)} %tile.2.row_ref, bf16[8,12288]{1,0:T(8,128)(2,1)S(1)} %copy-done.1), custom_call_target="tpu_custom_call" | custom-call | tf_op jit(solution)/shard_map/fill_sends/pallas_call | solution.py:165
  8.5 11.1 %all-to-all-start = ((bf16[128,8,768]{2,1,0:T(8,128)(2,1)}), bf16[128,8,768]{2,1,0:T(8,128)(2,1)S(1)}, u32[]{:S(2)}, u32[]{:S(2)}) async-start(bf16[128,8,768]{2,1,0:T(8,128)(2,1)} %bitcast.9), calls=%async_computation | async-start | bytes 3145728 | tf_op jit(solution)/shard_map/all_to_all | solution.py:456
  19.7 1.1 collective-permute-start
  20.8 0.8 collective-permute-start.1
  21.6 3.5 %collective-permute-start.3 = (bf16[2,1024,128]{2,1,0:T(8,128)(2,1)}, bf16[2,1024,128]{2,1,0:T(8,128)(2,1)}, u32[]{:S(2)}, u32[]{:S(2)}) collective-permute-start(bf16[2,1024,128]{2,1,0:T(8,128)(2,1)} %get-tuple-element.57), channel_id=1, source_target_pairs={{0,8},{1,9},{2,10},{3,11},{4,12},{5,13},{6,14},{7,15},{8,0},{9,1},... | collective-permute-start | bytes 1572872 | tf_op jit(solution)/shard_map/ppermute | solution.py:477
  25.1 0.9 collective-permute-start.5
  26.0 0.2 collective-permute-start.6
  26.2 24.8 %collective-permute-done.refs_2_ = bf16[2,1024,128]{2,1,0:T(8,128)(2,1)S(1)} collective-permute-done((bf16[2,1024,128]{2,1,0:T(8,128)(2,1)S(1)}, bf16[2,1024,128]{2,1,0:T(8,128)(2,1)S(1)}, u32[]{:S(2)}, u32[]{:S(2)}) %collective-permute-start) | collective-permute-done | bytes 524320 | tf_op jit(solution)/shard_map/ppermute | solution.py:477
  51.1 0.3 collective-permute-done.1.refs_3_
  51.4 0.8 copy-done.8
  52.2 8.6 %collective-permute-start.4 = (bf16[2,1024,128]{2,1,0:T(8,128)(2,1)}, bf16[2,1024,128]{2,1,0:T(8,128)(2,1)}, u32[]{:S(2)}, u32[]{:S(2)}) collective-permute-start(bf16[2,1024,128]{2,1,0:T(8,128)(2,1)} %get-tuple-element.58), channel_id=1, source_target_pairs={{0,18},{1,19},{2,16},{3,17},{4,22},{5,23},{6,20},{7,21},{8,26},{9,... | collective-permute-start | bytes 1572872 | tf_op jit(solution)/shard_map/ppermute | solution.py:477
  60.7 0.2 reshape.329
  61.0 5.6 %suffix.1 = (f32[8,8,16,128]{3,2,1,0:T(8,128)S(1)}, f32[8,8,16,128]{3,2,1,0:T(8,128)S(1)}) custom-call(s32[8,16]{1,0:T(8,128)S(1)} %copy-done.2, s32[8]{0:T(128)S(1)} %copy-done.3, bf16[8,8,16,128]{3,2,1,0:T(8,128)(2,1)S(1)} %pad.4.q_ref, bf16[128,16,2048]{2,1,0:T(8,128)(2,1)} %pool_ref.1), custom_call_target="tpu_custom_call" | custom-call | flops 1000000000 | bytes 9437184 | tf_op jit(solution)/shard_map/suffix/pallas_call | solution.py:215
  66.7 0.1 reshape.331.sl_ref
  66.8 2.4 %gather_rows.1 = (bf16[2,12,256,128]{3,2,1,0:T(8,128)(2,1)S(1)}, s32[8,1024]{1,0:T(8,128)S(1)}) custom-call(bf16[1024,768]{1,0:T(8,128)(2,1)S(1)} %bitcast.22), custom_call_target="tpu_custom_call" | custom-call | tf_op jit(solution)/shard_map/gather_rows/pallas_call | solution.py:265
  69.3 1.0 copy-done.5
  70.3 1.0 copy-done.9
  71.3 41.0 %prefix.1 = bf16[1024,896]{1,0:T(8,128)(2,1)} custom-call(bf16[2,12,256,128]{3,2,1,0:T(8,128)(2,1)S(1)} %get-tuple-element.51.q_ref, s32[8,1024]{1,0:T(8,128)S(1)} %get-tuple-element.52.place_ref, bf16[2,1024,128]{2,1,0:T(8,128)(2,1)S(1)} %copy-done.5, bf16[2,1024,128]{2,1,0:T(8,128)(2,1)} %collective-permute-done.2.refs_1_, ...), custom_call_target="tpu_custom_call" | custom-call | flops 20000000000 | bytes 8388608 | tf_op jit(solution)/shard_map/prefix/pallas_call | solution.py:391
  112.4 23.1 %all-to-all-start.1 = ((bf16[128,8,896]{2,1,0:T(8,128)(2,1)}), bf16[128,8,896]{2,1,0:T(8,128)(2,1)S(1)}, u32[]{:S(2)}, u32[]{:S(2)}) async-start(bf16[128,8,896]{2,1,0:T(8,128)(2,1)} %bitcast.25), calls=%async_computation.1 | async-start | bytes 3670016 | tf_op jit(solution)/shard_map/all_to_all | solution.py:456
  135.5 0.2 convert_reduce_fusion
  135.7 0.1 iota_select_fusion.1
  135.8 0.1 add_multiply_fusion
  135.9 0.1 multiply_add_fusion
  136.0 0.1 reshape.335.at_ref
  136.1 26.5 %all-to-all-done.1 = bf16[128,8,896]{2,1,0:T(8,128)(2,1)S(1)} async-done(((bf16[128,8,896]{2,1,0:T(8,128)(2,1)}), bf16[128,8,896]{2,1,0:T(8,128)(2,1)S(1)}, u32[]{:S(2)}, u32[]{:S(2)}) %all-to-all-start.1) | async-done | bytes 1835040 | tf_op jit(solution)/shard_map/all_to_all | solution.py:456
  162.6 2.2 %merge.1 = bf16[8,12288]{1,0:T(8,128)(2,1)} custom-call(s32[256,1]{1,0:T(8,128)S(1)} %reshape.335.at_ref, bf16[1024,896]{1,0:T(8,128)(2,1)S(1)} %bitcast.21, f32[8,12288]{1,0:T(8,128)S(1)} %reshape.330.so_ref, f32[8,12288]{1,0:T(8,128)S(1)} %reshape.331.sl_ref), custom_call_target="tpu_custom_call" | custom-call | tf_op jit(solution)/shard_map/merge/pallas_call | solution.py:446
  (31 shorter events, 0.2 us)
Async XLA Ops:
  0.1 2.2 %copy-start = (bf16[1,1024,2048]{2,1,0:T(8,128)(2,1)S(1)}, bf16[1,1024,2048]{2,1,0:T(8,128)(2,1)}, u32[]{:S(2)}) copy-start(bf16[1,1024,2048]{2,1,0:T(8,128)(2,1)} %kv_ref.1) | copy-start | bytes 12582916
  2.3 4.4 %copy-start.10 = (s32[8,1]{0,1:T(1,128)S(1)}, s32[8,1]{0,1:T(1,128)}, u32[]{:S(2)}) copy-start(s32[8,1]{0,1:T(1,128)} %param.7) | copy-start | bytes 100
  2.3 4.5 %copy-start.1 = (bf16[8,12288]{1,0:T(8,128)(2,1)S(1)}, bf16[8,12288]{1,0:T(8,128)(2,1)}, u32[]{:S(2)}) copy-start(bf16[8,12288]{1,0:T(8,128)(2,1)} %q_ref) | copy-start | bytes 589828
  5.8 0.8 copy-start.4
  8.5 52.5 %copy-start.2 = (s32[8,16]{1,0:T(8,128)S(1)}, s32[8,16]{1,0:T(8,128)}, u32[]{:S(2)}) copy-start(s32[8,16]{1,0:T(8,128)} %table_ref.1) | copy-start | bytes 1540
  8.5 52.5 %copy-start.3 = (s32[8]{0:T(128)S(1)}, s32[8]{0:T(128)}, u32[]{:S(2)}) copy-start(s32[8]{0:T(128)} %len_ref.1) | copy-start | bytes 100
  8.5 58.2 %all-to-all-start = ((bf16[128,8,768]{2,1,0:T(8,128)(2,1)}), bf16[128,8,768]{2,1,0:T(8,128)(2,1)S(1)}, u32[]{:S(2)}, u32[]{:S(2)}) async-start(bf16[128,8,768]{2,1,0:T(8,128)(2,1)} %bitcast.9), calls=%async_computation | async-start | bytes 3145728 | tf_op jit(solution)/shard_map/all_to_all | solution.py:456
  19.7 31.4 %collective-permute-start = (bf16[2,1024,128]{2,1,0:T(8,128)(2,1)S(1)}, bf16[2,1024,128]{2,1,0:T(8,128)(2,1)S(1)}, u32[]{:S(2)}, u32[]{:S(2)}) collective-permute-start(bf16[2,1024,128]{2,1,0:T(8,128)(2,1)S(1)} %get-tuple-element.43), channel_id=1, source_target_pairs={{0,4},{1,5},{2,6},{3,7},{4,8},{5,9},{6,10},{7,11},{8,12},{9,13},{1... | collective-permute-start | bytes 1572872 | tf_op jit(solution)/shard_map/ppermute | solution.py:477
  20.8 30.5 %collective-permute-start.1 = (bf16[2,1024,128]{2,1,0:T(8,128)(2,1)S(1)}, bf16[2,1024,128]{2,1,0:T(8,128)(2,1)S(1)}, u32[]{:S(2)}, u32[]{:S(2)}) collective-permute-start(bf16[2,1024,128]{2,1,0:T(8,128)(2,1)S(1)} %get-tuple-element.44), channel_id=1, source_target_pairs={{0,17},{1,18},{2,19},{3,16},{4,21},{5,22},{6,23},{7,20},{8,25},{9,... | collective-permute-start | bytes 1572872 | tf_op jit(solution)/shard_map/ppermute | solution.py:477
  21.6 47.6 %collective-permute-start.3 = (bf16[2,1024,128]{2,1,0:T(8,128)(2,1)}, bf16[2,1024,128]{2,1,0:T(8,128)(2,1)}, u32[]{:S(2)}, u32[]{:S(2)}) collective-permute-start(bf16[2,1024,128]{2,1,0:T(8,128)(2,1)} %get-tuple-element.57), channel_id=1, source_target_pairs={{0,8},{1,9},{2,10},{3,11},{4,12},{5,13},{6,14},{7,15},{8,0},{9,1},... | collective-permute-start | bytes 1572872 | tf_op jit(solution)/shard_map/ppermute | solution.py:477
  25.1 44.1 %collective-permute-start.5 = (bf16[2,1024,128]{2,1,0:T(8,128)(2,1)}, bf16[2,1024,128]{2,1,0:T(8,128)(2,1)}, u32[]{:S(2)}, u32[]{:S(2)}) collective-permute-start(bf16[2,1024,128]{2,1,0:T(8,128)(2,1)} %get-tuple-element.59), channel_id=1, source_target_pairs={{0,12},{1,13},{2,14},{3,15},{4,0},{5,1},{6,2},{7,3},{8,4},{9,5},{1... | collective-permute-start | bytes 1572872 | tf_op jit(solution)/shard_map/ppermute | solution.py:477
  26.0 43.2 %collective-permute-start.6 = (bf16[2,1024,128]{2,1,0:T(8,128)(2,1)}, bf16[2,1024,128]{2,1,0:T(8,128)(2,1)}, u32[]{:S(2)}, u32[]{:S(2)}) collective-permute-start(bf16[2,1024,128]{2,1,0:T(8,128)(2,1)} %get-tuple-element.60), channel_id=1, source_target_pairs={{0,19},{1,16},{2,17},{3,18},{4,23},{5,20},{6,21},{7,22},{8,27},{9,... | collective-permute-start | bytes 1572872 | tf_op jit(solution)/shard_map/ppermute | solution.py:477
  51.1 15.5 %copy-start.6 = (bf16[2,1024,128]{2,1,0:T(8,128)(2,1)}, bf16[2,1024,128]{2,1,0:T(8,128)(2,1)S(1)}, u32[]{:S(2)}) copy-start(bf16[2,1024,128]{2,1,0:T(8,128)(2,1)S(1)} %collective-permute-done.refs_2_) | copy-start | bytes 1572868
  51.4 0.8 copy-start.8
  52.2 17.1 %collective-permute-start.2 = (bf16[2,1024,128]{2,1,0:T(8,128)(2,1)}, bf16[2,1024,128]{2,1,0:T(8,128)(2,1)}, u32[]{:S(2)}, u32[]{:S(2)}) collective-permute-start(bf16[2,1024,128]{2,1,0:T(8,128)(2,1)} %get-tuple-element.54), channel_id=1, source_target_pairs={{0,16},{1,17},{2,18},{3,19},{4,20},{5,21},{6,22},{7,23},{8,24},{9,... | collective-permute-start | bytes 1572872 | tf_op jit(solution)/shard_map/ppermute | solution.py:477
  52.2 17.1 %collective-permute-start.4 = (bf16[2,1024,128]{2,1,0:T(8,128)(2,1)}, bf16[2,1024,128]{2,1,0:T(8,128)(2,1)}, u32[]{:S(2)}, u32[]{:S(2)}) collective-permute-start(bf16[2,1024,128]{2,1,0:T(8,128)(2,1)} %get-tuple-element.58), channel_id=1, source_target_pairs={{0,18},{1,19},{2,16},{3,17},{4,22},{5,23},{6,20},{7,21},{8,26},{9,... | collective-permute-start | bytes 1572872 | tf_op jit(solution)/shard_map/ppermute | solution.py:477
  66.7 2.6 %copy-start.7 = (bf16[2,1024,128]{2,1,0:T(8,128)(2,1)S(1)}, bf16[2,1024,128]{2,1,0:T(8,128)(2,1)}, u32[]{:S(2)}) copy-start(bf16[2,1024,128]{2,1,0:T(8,128)(2,1)} %copy-done.6) | copy-start | bytes 1572868
  69.3 1.0 copy-start.5
  70.3 1.0 copy-start.9
  112.4 50.2 %all-to-all-start.1 = ((bf16[128,8,896]{2,1,0:T(8,128)(2,1)}), bf16[128,8,896]{2,1,0:T(8,128)(2,1)S(1)}, u32[]{:S(2)}, u32[]{:S(2)}) async-start(bf16[128,8,896]{2,1,0:T(8,128)(2,1)} %bitcast.25), calls=%async_computation.1 | async-start | bytes 3670016 | tf_op jit(solution)/shard_map/all_to_all | solution.py:456

commit v3 on v2

--- a/solution.py
+++ b/solution.py
@@ -30,7 +30,6 @@
 ARR = DEVS * LINES
 HALF = DEVS * CAP
 TILE = 64
-CHUNK = 512
 STRIPS = 4
 EMPTY = 256.0
 SCALE = 1.0 / math.sqrt(HD)
@@ -273,98 +272,143 @@
     )(arrived)
 
 
-def prefix_kernel(q_ref, place_ref, *refs):
-    kv_refs = refs[:8]
-    out_ref, os, ls, ks, vs, sems = refs[8:]
-    copies = []
-    for n in range(8):
-        rows = pl.ds(n // 2 * BLOCK, BLOCK)
-        copies.append(
-            pltpu.make_async_copy(kv_refs[n].at[0], ks.at[n % 2, rows], sems.at[n, 0])
-        )
-        copies.append(
-            pltpu.make_async_copy(
-                kv_refs[n].at[1], vs.at[n % 2, rows, pl.ds(0, HD)], sems.at[n, 1]
-            )
-        )
-    for copy in copies:
-        copy.start()
-    vs[:, :, HD:] = jnp.ones((2, 4 * BLOCK, HD), BF16)
+def row_counts(place_ref):
+    line = iota((1, ARR), 1)
+    return [
+        jnp.max(jnp.where(line_turn(line) == turn, place_ref[0:1], -1)) + 1
+        for turn in range(2)
+    ]
+
+
+def widen(column):
+    column = column.reshape(GROUP, TILE, 1)
+    lane = iota((TILE, HD), 1)
+    wide = jnp.zeros((TILE, HD), F32)
+    for g in range(GROUP):
+        mine = (lane == g) | (lane == g + GROUP) | (lane == g + 2 * GROUP)
+        wide = wide + jnp.where(mine, column[g], 0.0)
+    return wide
+
+
+def plain_part(q, keys, values):
+    strip = GROUP * TILE // STRIPS
+    outs, totals = [], []
+    for i in range(STRIPS):
+        score = dot_t(q[i * strip : (i + 1) * strip], keys)
+        weights = jnp.exp2(score * FACTOR)
+        cuts = [weights[:, c : c + HD] for c in range(0, weights.shape[1], HD)]
+        totals.append(jnp.sum(functools.reduce(jnp.add, cuts), axis=1, keepdims=True))
+        outs.append(dot(weights.astype(BF16), values))
+    out = jnp.concatenate(outs, axis=0).reshape(GROUP, TILE, HD)
+    return out, widen(jnp.concatenate(totals, axis=0))
+
+
+def tile_part(q_ref, kv_refs, turn, at):
+    q = q_ref[turn, :, pl.ds(at, TILE), :].reshape(GROUP * TILE, HD)
+    mine = kv_refs[turn::2]
+    keys = jnp.concatenate([ref[0] for ref in mine], axis=0)
+    values = jnp.concatenate([ref[1] for ref in mine], axis=0)
+    return plain_part(q, keys, values)
+
+
+def over_tiles(count, step):
+    def tile(t, carry):
+        step(pl.multiple_of(t * TILE, TILE))
+        return carry
+
+    lax.fori_loop(0, (count + TILE - 1) // TILE, tile, 0)
+
+
+def sums_kernel(blocks, first, q_ref, place_ref, *refs):
+    kv_refs, refs = refs[: 2 * blocks], refs[2 * blocks :]
+    out_ref, total_ref = refs[-2:]
+    for turn, count in enumerate(row_counts(place_ref)):
+
+        def step(at, turn=turn):
+            out, total = tile_part(q_ref, kv_refs, turn, at)
+            if not first:
+                out = out + refs[0][turn, :, pl.ds(at, TILE), :]
+                total = total + refs[1][turn, pl.ds(at, TILE), :]
+            out_ref[turn, :, pl.ds(at, TILE), :] = out
+            total_ref[turn, pl.ds(at, TILE), :] = total
+
+        over_tiles(count, step)
+
+
+def add_sums(rows, place, kv, state):
+    blocks = len(kv) // 2
+    vmem = pl.BlockSpec(memory_space=pltpu.VMEM)
+    return pl.pallas_call(
+        functools.partial(sums_kernel, blocks, not state),
+        out_shape=[
+            jax.ShapeDtypeStruct((2, GROUP, HALF, HD), F32),
+            jax.ShapeDtypeStruct((2, HALF, HD), F32),
+        ],
+        in_specs=[vmem] * (2 + len(kv) + len(state)),
+        out_specs=[vmem, vmem],
+        compiler_params=pltpu.CompilerParams(vmem_limit_bytes=32 * MB),
+        cost_estimate=pl.CostEstimate(
+            flops=blocks * 4 * 10**9, bytes_accessed=8 * MB, transcendentals=0
+        ),
+        name="sums_%d" % blocks,
+    )(rows, place, *kv, *state)
+
+
+def last_kernel(q_ref, place_ref, sum_ref, total_ref, *refs):
+    kv_refs, all_refs, (out_ref, os, ls, held, sems) = refs[:2], refs[2:10], refs[10:]
     for turn in range(2):
         os[turn] = jnp.zeros((GROUP // 2, HALF, 2 * HD), BF16)
         ls[turn] = jnp.zeros((HALF, HD), BF16)
-    place = place_ref[...]
-    line = iota((1, ARR), 1)
-    counts = [
-        jnp.max(jnp.where(line_turn(line) == turn, place[0:1], -1)) + 1 for turn in range(2)
-    ]
-    for copy in copies:
-        copy.wait()
-    high_rows = GROUP * TILE
-    strip = high_rows // STRIPS
-
-    def finish(turn, at, acc, shift):
-        total = acc[:, HD : HD + 1]
-        out = (acc[:, :HD] / total).astype(BF16).reshape(GROUP, TILE, HD)
+    lane = iota((TILE, HD), 1)
+
+    def finish(turn, at, out, total, shift):
         for g in range(GROUP):
-            os[turn, g // 2, pl.ds(at, TILE), g % 2 * HD : (g % 2 + 1) * HD] = out[g]
-        lse = (shift + jnp.log(total)).reshape(GROUP, TILE, 1)
-        lane = iota((TILE, HD), 1)
-        wide = jnp.zeros((TILE, HD), F32)
-        for g in range(GROUP):
-            mine = (lane == g) | (lane == g + GROUP) | (lane == g + 2 * GROUP)
-            wide = wide + jnp.where(mine, lse[g], 0.0)
-        one = wide.astype(BF16).astype(F32)
-        two = (wide - one).astype(BF16).astype(F32)
-        three = wide - one - two
+            os[turn, g // 2, pl.ds(at, TILE), g % 2 * HD : (g % 2 + 1) * HD] = (
+                out[g] / total[:, g : g + 1]
+            ).astype(BF16)
+        lse = jnp.where(lane < 3 * GROUP, shift + jnp.log(total), 0.0)
+        one = lse.astype(BF16).astype(F32)
+        two = (lse - one).astype(BF16).astype(F32)
+        three = lse - one - two
         split = jnp.where(lane < GROUP, one, jnp.where(lane < 2 * GROUP, two, three))
         ls[turn, pl.ds(at, TILE), :] = split.astype(BF16)
 
-    for turn in range(2):
-
-        def tile(t, carry, turn=turn):
-            at = pl.multiple_of(t * TILE, TILE)
-            q = q_ref[turn, :, pl.ds(at, TILE), :].reshape(high_rows, HD)
-            accs = []
-            for i in range(STRIPS):
-                part_q = q[i * strip : (i + 1) * strip]
-                acc = None
-                score = dot_t(part_q, ks[turn, :CHUNK, :])
-                for j in range(4 * BLOCK // CHUNK):
-                    after = None
-                    if (j + 1) * CHUNK < 4 * BLOCK:
-                        after = dot_t(part_q, ks[turn, (j + 1) * CHUNK : (j + 2) * CHUNK, :])
-                    weights = jnp.exp2(score * FACTOR).astype(BF16)
-                    part = dot(weights, vs[turn, j * CHUNK : (j + 1) * CHUNK, :])
-                    acc = part if acc is None else acc + part
-                    score = after
-                accs.append(acc)
-            acc = jnp.concatenate(accs, axis=0)
-            finish(turn, at, acc, 0.0)
-            total = acc[:, HD : HD + 1]
-            plain = (jnp.min(total) > LEAST) & (jnp.max(total) < MOST)
+    for turn, count in enumerate(row_counts(place_ref)):
+
+        def step(at, turn=turn):
+            out, total = tile_part(q_ref, kv_refs, turn, at)
+            out = out + sum_ref[turn, :, pl.ds(at, TILE), :]
+            total = total + total_ref[turn, pl.ds(at, TILE), :]
+            finish(turn, at, out, total, 0.0)
+            known = jnp.where(lane < 3 * GROUP, total, 1.0)
+            plain = (jnp.min(known) > LEAST) & (jnp.max(known) < MOST)
 
             @pl.when(jnp.logical_not(plain))
             def _():
-                top = acc = None
+                q = q_ref[turn, :, pl.ds(at, TILE), :].reshape(GROUP * TILE, HD)
+                top = amount = acc = None
                 for k in range(4):
-                    rows = slice(k * BLOCK, (k + 1) * BLOCK)
-                    score = dot_t(q, ks[turn, rows, :])
+                    copy = pltpu.make_async_copy(all_refs[k * 2 + turn], held, sems.at[0])
+                    copy.start()
+                    copy.wait()
+                    score = dot_t(q, held[0])
                     high = jnp.max(score, axis=1, keepdims=True)
                     if k > 0:
                         high = jnp.maximum(top, high)
-                    weights = jnp.exp2(score * FACTOR - high * FACTOR).astype(BF16)
-                    part = dot(weights, vs[turn, rows, :])
+                    weights = jnp.exp2(score * FACTOR - high * FACTOR)
+                    part_amount = jnp.sum(weights, axis=1, keepdims=True)
+                    part = dot(weights.astype(BF16), held[1])
                     if k > 0:
-                        part = acc * jnp.exp2((top - high) * FACTOR) + part
-                    top, acc = high, part
-                finish(turn, at, acc, top * SCALE)
-
-            return carry
-
-        lax.fori_loop(0, (counts[turn] + TILE - 1) // TILE, tile, 0)
-
-    place_col = jnp.transpose(place.astype(F32))[:, 0:1].astype(jnp.int32)
+                        fade = jnp.exp2((top - high) * FACTOR)
+                        part = acc * fade + part
+                        part_amount = amount * fade + part_amount
+                    top, amount, acc = high, part_amount, part
+                acc = acc.reshape(GROUP, TILE, HD)
+                finish(turn, at, acc, widen(amount), widen(top * SCALE))
+
+        over_tiles(count, step)
+
+    place_col = jnp.transpose(place_ref[...].astype(F32))[:, 0:1].astype(jnp.int32)
     line = iota((ARR, 1), 0)
     scatter = jnp.concatenate(
         [
@@ -386,26 +430,24 @@
     out_ref[:, PART:] = dot(scatter, source).astype(BF16)
 
 
-def prefix(arrived, kv):
-    rows, place = gather_rows(arrived)
+def finish_prefix(rows, place, state, last, everything):
+    vmem = pl.BlockSpec(memory_space=pltpu.VMEM)
     return pl.pallas_call(
-        prefix_kernel,
+        last_kernel,
         out_shape=jax.ShapeDtypeStruct((ARR, PART + HD), BF16),
-        in_specs=[pl.BlockSpec(memory_space=pltpu.VMEM)] * 2
-        + [pl.BlockSpec(memory_space=pl.ANY)] * 8,
+        in_specs=[vmem] * 6 + [pl.BlockSpec(memory_space=pl.ANY)] * 8,
         scratch_shapes=[
             pltpu.VMEM((2, GROUP // 2, HALF, 2 * HD), BF16),
             pltpu.VMEM((2, HALF, HD), BF16),
-            pltpu.VMEM((2, 4 * BLOCK, HD), BF16),
-            pltpu.VMEM((2, 4 * BLOCK, 2 * HD), BF16),
-            pltpu.SemaphoreType.DMA((8, 2)),
+            pltpu.VMEM((2, BLOCK, HD), BF16),
+            pltpu.SemaphoreType.DMA((1,)),
         ],
-        compiler_params=pltpu.CompilerParams(vmem_limit_bytes=48 * MB),
+        compiler_params=pltpu.CompilerParams(vmem_limit_bytes=36 * MB),
         cost_estimate=pl.CostEstimate(
-            flops=20 * 10**9, bytes_accessed=8 * MB, transcendentals=0
+            flops=6 * 10**9, bytes_accessed=8 * MB, transcendentals=0
         ),
-        name="prefix",
-    )(rows, place, *kv)
+        name="finish_prefix",
+    )(rows, place, *state, *last, *everything)
 
 
 def merge_kernel(at_ref, back_ref, so_ref, sl_ref, out_ref):
@@ -470,24 +512,29 @@
             for cross in range(2)
         ]
     ).astype(jnp.int32)
+    sends = fill_sends(prompt_ids, queries)
+    sends, prefix_kv = lax.optimization_barrier((sends, prefix_kv))
+    arrived = exchange(sends)
     pieces = split_heads(heads, prefix_kv)
-    pieces, queries = lax.optimization_barrier((pieces, queries))
 
     def move(n, piece):
         return lax.ppermute(piece, AXES, routes(n // 2, n % 2))
 
     kv = list(pieces)
-    for n in (2, 3, 6, 7, 4):
+    for n in (2, 3, 6, 7, 1):
         kv[n] = move(n, pieces[n])
-    arrived = exchange(fill_sends(prompt_ids, queries))
-    kv[2], kv[3], late, last, queries = lax.optimization_barrier(
-        (kv[2], kv[3], pieces[5], pieces[1], queries)
-    )
-    kv[5] = move(5, late)
-    kv[1] = move(1, last)
+    kv[1], later, queries = lax.optimization_barrier((kv[1], pieces[4], queries))
+    kv[4] = move(4, later)
     so, sl = suffix(page_table, suffix_len, queries, suffix_pool)
     arrived, so, sl = lax.optimization_barrier((arrived, so, sl))
-    back = exchange(prefix(arrived, kv))
+    rows, place = gather_rows(arrived)
+    state = add_sums(rows, place, kv[0:2], ())
+    state, kv[2], kv[3], kv[6], kv[7], later = lax.optimization_barrier(
+        (state, kv[2], kv[3], kv[6], kv[7], pieces[5])
+    )
+    kv[5] = move(5, later)
+    state = add_sums(rows, place, kv[2:4] + kv[6:8], state)
+    back = exchange(finish_prefix(rows, place, state, kv[4:6], kv))
     return merge(prompt_ids, back, so, sl)
 
 

time: 165 us -> 164 us (level)
  waiting for transfers between devices: 51.6 us -> 28.2 us
  Pallas kernels: 56.5 us -> 70.2 us
  local copies, waits for them, and re-layouts: 6.57 us -> 10.3 us
  starting transfers between devices: 49.4 us -> 53.1 us
    ppermute x7, waiting for transfers between devices: 25.1 us -> 0.58 us  [move(): return lax.ppermute(piece, AXES, routes(n // 2, n % 2))]
    pallas_call x1 -> x3, Pallas kernels: 41 us -> 54.9 us  [the longest x1 40.2 us: finish_prefix(): pl.pallas_call(last_kernel, out_shape=jax.ShapeDtypeStruct((ARR, PART + H...]
    all_to_all x2, starting transfers between devices: 34.3 us -> 41.6 us  [exchange(): lax.all_to_all(array.reshape(DEVS, LINES, width), AXES, split_axis=0, con...]
    ppermute x7, starting transfers between devices: 15.1 us -> 11.5 us  [move(): return lax.ppermute(piece, AXES, routes(n // 2, n % 2))]
    unnamed x23 -> x29, local copies, waits for them, and re-layouts: 5.97 us -> 7.54 us
  transfers between devices with their start and end apart: 9 -> 9, of which waited for: 3 -> 4; matrix products, arithmetic and copies ran while one was open for 1% -> 2% of each run, Pallas kernels for 5% -> 16%
where the time goes in v3:
time: 164 us; the launch traced here: 163 us
  Pallas kernels  70.2 us (43%)
  starting transfers between devices  53.1 us (32%)
  waiting for transfers between devices  28.2 us (17%)
  local copies, waits for them, and re-layouts  10.3 us (6%)
    all_to_all x2, starting transfers between devices, exchange(): lax.all_to_all(array.reshape(DEVS, LINES, width), AXES, split_axis=0, con...  41.6 us
    pallas_call x1, Pallas kernels, finish_prefix(): pl.pallas_call(last_kernel, out_shape=jax.ShapeDtypeStruct((ARR, PART + H...  40.2 us
    all_to_all x2, waiting for transfers between devices, exchange(): lax.all_to_all(array.reshape(DEVS, LINES, width), AXES, split_axis=0, con...  27.7 us
    pallas_call x2, Pallas kernels, add_sums(): pl.pallas_call(functools.partial(sums_kernel, blocks, not state), out_sha...  14.7 us
    ppermute x7, starting transfers between devices, move(): return lax.ppermute(piece, AXES, routes(n // 2, n % 2))  11.5 us
    unnamed x29, local copies, waits for them, and re-layouts  7.54 us
    pallas_call x1, Pallas kernels, suffix(): pl.pallas_call(suffix_kernel, out_shape=[shape, shape], in_specs=[smem, s...  5.6 us
    pallas_call x1, Pallas kernels, split_heads(): pl.pallas_call(split_heads_kernel, out_shape=[jax.ShapeDtypeStruct((2, BL...  3.35 us
  transfers between devices with their start and end apart: 9, of which 4 were waited for; matrix products, arithmetic and copies ran while one was open for 2% of the time, Pallas kernels for 16%

profile of v3, /device:TPU:0, one launch (start us, length us, event | category | flops | bytes accessed | tf_op | source)
XLA Modules:
  0.0 162.7 jit_solution(2894034169457649785)
XLA Ops:
  0.0 0.7 copy.8.col_ref
  0.7 0.7 eq.59
  1.5 0.9 copy-done.4
  2.4 1.7 %fill_sends.1 = bf16[1024,768]{1,0:T(8,128)(2,1)} custom-call(s32[8,1]{1,0:T(8,128)S(1)} %copy.8.col_ref, s32[1,64]{1,0:T(1,128)S(1)} %tile.2.row_ref, bf16[8,12288]{1,0:T(8,128)(2,1)S(1)} %copy-done.4), custom_call_target="tpu_custom_call" | custom-call | tf_op jit(solution)/shard_map/fill_sends/pallas_call | solution.py:164
  4.1 11.1 %all-to-all-start = ((bf16[128,8,768]{2,1,0:T(8,128)(2,1)}), bf16[128,8,768]{2,1,0:T(8,128)(2,1)S(1)}, u32[]{:S(2)}, u32[]{:S(2)}) async-start(bf16[128,8,768]{2,1,0:T(8,128)(2,1)} %bitcast.1), calls=%async_computation | async-start | bytes 3145728 | tf_op jit(solution)/shard_map/all_to_all | solution.py:498
  15.5 2.2 %copy-done = bf16[1,1024,2048]{2,1,0:T(8,128)(2,1)S(1)} copy-done((bf16[1,1024,2048]{2,1,0:T(8,128)(2,1)S(1)}, bf16[1,1024,2048]{2,1,0:T(8,128)(2,1)}, u32[]{:S(2)}) %copy-start) | copy-done | bytes 4194328
  17.7 3.4 %split_heads.1 = (bf16[2,1024,128]{2,1,0:T(8,128)(2,1)S(1)}, bf16[2,1024,128]{2,1,0:T(8,128)(2,1)S(1)}, bf16[2,1024,128]{2,1,0:T(8,128)(2,1)}, bf16[2,1024,128]{...) custom-call(s32[8]{0:T(128)S(1)} %stack.35.head_ref, ...), custom_call_target="tpu_custom_call" | custom-call | tf_op jit(solution)/shard_map/split_heads/pallas_call | solution.py:100
  21.1 0.8 copy-done.10
  21.9 0.8 copy-done.12
  22.7 1.2 collective-permute-start.1
  23.9 1.0 collective-permute-start.2
  24.9 3.5 %collective-permute-start.3 = (bf16[2,1024,128]{2,1,0:T(8,128)(2,1)}, bf16[2,1024,128]{2,1,0:T(8,128)(2,1)}, u32[]{:S(2)}, u32[]{:S(2)}) collective-permute-start(bf16[2,1024,128]{2,1,0:T(8,128)(2,1)} %get-tuple-element.52), channel_id=1, source_target_pairs={{0,12},{1,13},{2,14},{3,15},{4,0},{5,1},{6,2},{7,3},{8,4},{9,5},{1... | collective-permute-start | bytes 1572872 | tf_op jit(solution)/shard_map/ppermute | solution.py:521
  28.4 0.3 collective-permute-start.4
  28.7 0.8 copy-done.8
  29.5 0.2 reshape.329
  29.8 5.6 %suffix.1 = (f32[8,8,16,128]{3,2,1,0:T(8,128)S(1)}, f32[8,8,16,128]{3,2,1,0:T(8,128)S(1)}) custom-call(s32[8,16]{1,0:T(8,128)S(1)} %copy-done.6, s32[8]{0:T(128)S(1)} %copy-done.7, bf16[8,8,16,128]{3,2,1,0:T(8,128)(2,1)S(1)} %pad.4.q_ref, bf16[128,16,2048]{2,1,0:T(8,128)(2,1)} %pool_ref.1), custom_call_target="tpu_custom_call" | custom-call | flops 1000000000 | bytes 9437184 | tf_op jit(solution)/shard_map/suffix/pallas_call | solution.py:214
  35.4 0.8 reshape.330.so_ref
  36.2 0.9 reshape.331.sl_ref
  37.0 1.5 collective-permute-start.5
  38.6 1.2 all-to-all-done
  39.7 2.4 %gather_rows.1 = (bf16[2,12,256,128]{3,2,1,0:T(8,128)(2,1)S(1)}, s32[8,1024]{1,0:T(8,128)S(1)}) custom-call(bf16[1024,768]{1,0:T(8,128)(2,1)S(1)} %bitcast.22), custom_call_target="tpu_custom_call" | custom-call | tf_op jit(solution)/shard_map/gather_rows/pallas_call | solution.py:264
  42.2 5.3 %sums_1.1 = (f32[2,12,256,128]{3,2,1,0:T(8,128)S(1)}, f32[2,256,128]{2,1,0:T(8,128)S(1)}) custom-call(bf16[2,12,256,128]{3,2,1,0:T(8,128)(2,1)S(1)} %get-tuple-element.44.q_ref, s32[8,1024]{1,0:T(8,128)S(1)} %get-tuple-element.45.place_ref, bf16[2,1024,128]{2,1,0:T(8,128)(2,1)S(1)} %get-tuple-element.46.refs_0_.refs_2_, bf16[2,1024,128]{2,1,0:T(8,128)(2,1)S(1)} %copy-done.9), custom_call_target="tpu_custom_call" | custom-call | flops 4000000000 | bytes 8388608 | tf_op jit(solution)/shard_map/sums_1/pallas_call | solution.py:341
  47.5 0.4 collective-permute-done.1.refs_0_.refs_4_
  47.9 0.2 collective-permute-done.2.refs_1_.refs_5_
  48.1 4.0 %collective-permute-start.6 = (bf16[2,1024,128]{2,1,0:T(8,128)(2,1)S(1)}, bf16[2,1024,128]{2,1,0:T(8,128)(2,1)S(1)}, u32[]{:S(2)}, u32[]{:S(2)}) collective-permute-start(bf16[2,1024,128]{2,1,0:T(8,128)(2,1)S(1)} %copy-done.11), channel_id=1, source_target_pairs={{0,18},{1,19},{2,16},{3,17},{4,22},{5,23},{6,20},{7,21},{8,26},{9,... | collective-permute-start | bytes 1572872 | tf_op jit(solution)/shard_map/ppermute | solution.py:521
  52.0 9.4 %sums_2.1 = (f32[2,12,256,128]{3,2,1,0:T(8,128)S(1)}, f32[2,256,128]{2,1,0:T(8,128)S(1)}) custom-call(bf16[2,12,256,128]{3,2,1,0:T(8,128)(2,1)S(1)} %get-tuple-element.44.q_ref, s32[8,1024]{1,0:T(8,128)S(1)} %get-tuple-element.45.place_ref, bf16[2,1024,128]{2,1,0:T(8,128)(2,1)} %collective-permute-done.1.refs_0_.refs_4_, ...), custom_call_target="tpu_custom_call" | custom-call | flops 8000000000 | bytes 8388608 | tf_op jit(solution)/shard_map/sums_2/pallas_call | solution.py:341
  61.5 40.2 %finish_prefix.1 = bf16[1024,896]{1,0:T(8,128)(2,1)S(1)} custom-call(bf16[2,12,256,128]{3,2,1,0:T(8,128)(2,1)S(1)} %get-tuple-element.44.q_ref, s32[8,1024]{1,0:T(8,128)S(1)} %get-tuple-element.45.place_ref, f32[2,12,256,128]{3,2,1,0:T(8,128)S(1)} %get-tuple-element.61.sum_ref, f32[2,256,128]{2,1,0:T(8,128)S(1)} %get-tuple-element.62.total_ref, ...), custom_call_target="tpu_custom_call" | custom-call | flops 6000000000 | bytes 8388608 | tf_op jit(solution)/shard_map/finish_prefix/pallas_call | solution.py:435
  101.7 1.3 copy-done.1
  102.9 30.4 %all-to-all-start.1 = ((bf16[128,8,896]{2,1,0:T(8,128)(2,1)}), bf16[128,8,896]{2,1,0:T(8,128)(2,1)S(1)}, u32[]{:S(2)}, u32[]{:S(2)}) async-start(bf16[128,8,896]{2,1,0:T(8,128)(2,1)} %bitcast.23), calls=%async_computation.1 | async-start | bytes 3670016 | tf_op jit(solution)/shard_map/all_to_all | solution.py:498
  133.4 0.2 convert_reduce_fusion
  134.0 26.5 %all-to-all-done.1 = bf16[128,8,896]{2,1,0:T(8,128)(2,1)S(1)} async-done(((bf16[128,8,896]{2,1,0:T(8,128)(2,1)}), bf16[128,8,896]{2,1,0:T(8,128)(2,1)S(1)}, u32[]{:S(2)}, u32[]{:S(2)}) %all-to-all-start.1) | async-done | bytes 1835040 | tf_op jit(solution)/shard_map/all_to_all | solution.py:498
  160.5 2.2 %merge.1 = bf16[8,12288]{1,0:T(8,128)(2,1)} custom-call(s32[256,1]{1,0:T(8,128)S(1)} %reshape.335.at_ref, bf16[1024,896]{1,0:T(8,128)(2,1)S(1)} %bitcast.21, f32[8,12288]{1,0:T(8,128)S(1)} %copy-done.2, f32[8,12288]{1,0:T(8,128)S(1)} %copy-done.3), custom_call_target="tpu_custom_call" | custom-call | tf_op jit(solution)/shard_map/merge/pallas_call | solution.py:488
  (38 shorter events, 0.6 us)
Async XLA Ops:
  1.5 0.9 copy-start.4
  4.1 35.6 %all-to-all-start = ((bf16[128,8,768]{2,1,0:T(8,128)(2,1)}), bf16[128,8,768]{2,1,0:T(8,128)(2,1)S(1)}, u32[]{:S(2)}, u32[]{:S(2)}) async-start(bf16[128,8,768]{2,1,0:T(8,128)(2,1)} %bitcast.1), calls=%async_computation | async-start | bytes 3145728 | tf_op jit(solution)/shard_map/all_to_all | solution.py:498
  15.5 2.2 %copy-start = (bf16[1,1024,2048]{2,1,0:T(8,128)(2,1)S(1)}, bf16[1,1024,2048]{2,1,0:T(8,128)(2,1)}, u32[]{:S(2)}) copy-start(bf16[1,1024,2048]{2,1,0:T(8,128)(2,1)} %kv_ref) | copy-start | bytes 12582916
  17.7 11.9 %copy-start.5 = (bf16[8,12288]{1,0:T(8,128)(2,1)S(1)}, bf16[8,12288]{1,0:T(8,128)(2,1)}, u32[]{:S(2)}) copy-start(bf16[8,12288]{1,0:T(8,128)(2,1)} %q_ref.1) | copy-start | bytes 589828
  17.7 12.1 %copy-start.6 = (s32[8,16]{1,0:T(8,128)S(1)}, s32[8,16]{1,0:T(8,128)}, u32[]{:S(2)}) copy-start(s32[8,16]{1,0:T(8,128)} %table_ref.1) | copy-start | bytes 1540
  17.7 12.1 %copy-start.7 = (s32[8]{0:T(128)S(1)}, s32[8]{0:T(128)}, u32[]{:S(2)}) copy-start(s32[8]{0:T(128)} %len_ref.1) | copy-start | bytes 100
  21.0 0.8 copy-start.10
  21.9 0.8 copy-start.12
  22.7 6.1 %collective-permute-start = (bf16[2,1024,128]{2,1,0:T(8,128)(2,1)S(1)}, bf16[2,1024,128]{2,1,0:T(8,128)(2,1)S(1)}, u32[]{:S(2)}, u32[]{:S(2)}) collective-permute-start(bf16[2,1024,128]{2,1,0:T(8,128)(2,1)S(1)} %get-tuple-element.38), channel_id=1, source_target_pairs={{0,16},{1,17},{2,18},{3,19},{4,20},{5,21},{6,22},{7,23},{8,24},{9,... | collective-permute-start | bytes 1572872 | tf_op jit(solution)/shard_map/ppermute | solution.py:521
  22.7 25.2 %collective-permute-start.1 = (bf16[2,1024,128]{2,1,0:T(8,128)(2,1)}, bf16[2,1024,128]{2,1,0:T(8,128)(2,1)}, u32[]{:S(2)}, u32[]{:S(2)}) collective-permute-start(bf16[2,1024,128]{2,1,0:T(8,128)(2,1)} %get-tuple-element.50), channel_id=1, source_target_pairs={{0,4},{1,5},{2,6},{3,7},{4,8},{5,9},{6,10},{7,11},{8,12},{9,13},{1... | collective-permute-start | bytes 1572872 | tf_op jit(solution)/shard_map/ppermute | solution.py:521
  23.9 24.2 %collective-permute-start.2 = (bf16[2,1024,128]{2,1,0:T(8,128)(2,1)}, bf16[2,1024,128]{2,1,0:T(8,128)(2,1)}, u32[]{:S(2)}, u32[]{:S(2)}) collective-permute-start(bf16[2,1024,128]{2,1,0:T(8,128)(2,1)} %get-tuple-element.51), channel_id=1, source_target_pairs={{0,17},{1,18},{2,19},{3,16},{4,21},{5,22},{6,23},{7,20},{8,25},{9,... | collective-permute-start | bytes 1572872 | tf_op jit(solution)/shard_map/ppermute | solution.py:521
  24.9 23.1 %collective-permute-start.3 = (bf16[2,1024,128]{2,1,0:T(8,128)(2,1)}, bf16[2,1024,128]{2,1,0:T(8,128)(2,1)}, u32[]{:S(2)}, u32[]{:S(2)}) collective-permute-start(bf16[2,1024,128]{2,1,0:T(8,128)(2,1)} %get-tuple-element.52), channel_id=1, source_target_pairs={{0,12},{1,13},{2,14},{3,15},{4,0},{5,1},{6,2},{7,3},{8,4},{9,5},{1... | collective-permute-start | bytes 1572872 | tf_op jit(solution)/shard_map/ppermute | solution.py:521
  28.4 19.7 %collective-permute-start.4 = (bf16[2,1024,128]{2,1,0:T(8,128)(2,1)}, bf16[2,1024,128]{2,1,0:T(8,128)(2,1)}, u32[]{:S(2)}, u32[]{:S(2)}) collective-permute-start(bf16[2,1024,128]{2,1,0:T(8,128)(2,1)} %get-tuple-element.53), channel_id=1, source_target_pairs={{0,19},{1,16},{2,17},{3,18},{4,23},{5,20},{6,21},{7,22},{8,27},{9,... | collective-permute-start | bytes 1572872 | tf_op jit(solution)/shard_map/ppermute | solution.py:521
  28.7 0.8 copy-start.8
  36.2 6.0 %copy-start.9 = (bf16[2,1024,128]{2,1,0:T(8,128)(2,1)S(1)}, bf16[2,1024,128]{2,1,0:T(8,128)(2,1)}, u32[]{:S(2)}) copy-start(bf16[2,1024,128]{2,1,0:T(8,128)(2,1)} %copy-done.8) | copy-start | bytes 1572868
  37.0 24.4 %collective-permute-start.5 = (bf16[2,1024,128]{2,1,0:T(8,128)(2,1)}, bf16[2,1024,128]{2,1,0:T(8,128)(2,1)S(1)}, u32[]{:S(2)}, u32[]{:S(2)}) collective-permute-start(bf16[2,1024,128]{2,1,0:T(8,128)(2,1)} %copy-done.12), channel_id=1, source_target_pairs={{0,8},{1,9},{2,10},{3,11},{4,12},{5,13},{6,14},{7,15},{8,0},{9,1},... | collective-permute-start | bytes 1572872 | tf_op jit(solution)/shard_map/ppermute | solution.py:521
  42.2 5.9 %copy-start.11 = (bf16[2,1024,128]{2,1,0:T(8,128)(2,1)S(1)}, bf16[2,1024,128]{2,1,0:T(8,128)(2,1)}, u32[]{:S(2)}) copy-start(bf16[2,1024,128]{2,1,0:T(8,128)(2,1)} %copy-done.10) | copy-start | bytes 1572868
  48.1 13.4 %collective-permute-start.6 = (bf16[2,1024,128]{2,1,0:T(8,128)(2,1)S(1)}, bf16[2,1024,128]{2,1,0:T(8,128)(2,1)S(1)}, u32[]{:S(2)}, u32[]{:S(2)}) collective-permute-start(bf16[2,1024,128]{2,1,0:T(8,128)(2,1)S(1)} %copy-done.11), channel_id=1, source_target_pairs={{0,18},{1,19},{2,16},{3,17},{4,22},{5,23},{6,20},{7,21},{8,26},{9,... | collective-permute-start | bytes 1572872 | tf_op jit(solution)/shard_map/ppermute | solution.py:521
  101.7 1.3 copy-start.1
  102.9 30.5 %copy-start.13 = (s32[8,1]{0,1:T(1,128)S(1)}, s32[8,1]{0,1:T(1,128)}, u32[]{:S(2)}) copy-start(s32[8,1]{0,1:T(1,128)} %param.7) | copy-start | bytes 100
  102.9 57.5 %copy-start.2 = (f32[8,12288]{1,0:T(8,128)S(1)}, f32[8,12288]{1,0:T(8,128)}, u32[]{:S(2)}) copy-start(f32[8,12288]{1,0:T(8,128)} %reshape.330.so_ref) | copy-start | bytes 1179652
  102.9 57.5 %copy-start.3 = (f32[8,12288]{1,0:T(8,128)S(1)}, f32[8,12288]{1,0:T(8,128)}, u32[]{:S(2)}) copy-start(f32[8,12288]{1,0:T(8,128)} %reshape.331.sl_ref) | copy-start | bytes 1179652
  102.9 57.5 %all-to-all-start.1 = ((bf16[128,8,896]{2,1,0:T(8,128)(2,1)}), bf16[128,8,896]{2,1,0:T(8,128)(2,1)S(1)}, u32[]{:S(2)}, u32[]{:S(2)}) async-start(bf16[128,8,896]{2,1,0:T(8,128)(2,1)} %bitcast.23), calls=%async_computation.1 | async-start | bytes 3670016 | tf_op jit(solution)/shard_map/all_to_all | solution.py:498

commit v4 on v3

--- a/solution.py
+++ b/solution.py
@@ -100,24 +100,24 @@
     return pl.pallas_call(
         split_heads_kernel,
         out_shape=[jax.ShapeDtypeStruct((2, BLOCK, HD), BF16)] * n,
-        in_specs=[pl.BlockSpec(memory_space=pltpu.SMEM), pl.BlockSpec(memory_space=pl.ANY)],
-        out_specs=[pl.BlockSpec(memory_space=pl.ANY)] * n,
+        in_specs=[pl.BlockSpec(memory_space=pltpu.SMEM), pl.BlockSpec(memory_space=pltpu.HBM)],
+        out_specs=[pl.BlockSpec(memory_space=pltpu.HBM)] * n,
         scratch_shapes=[
             pltpu.VMEM((n, 2, BLOCK, HD), BF16),
             pltpu.SemaphoreType.DMA((2, n, 2)),
         ],
-        compiler_params=pltpu.CompilerParams(vmem_limit_bytes=16 * MB),
+        compiler_params=pltpu.CompilerParams(vmem_limit_bytes=8 * MB),
         name="split_heads",
     )(heads, prefix_kv)
 
 
-def send_kernel(col_ref, row_ref, q_ref, out_ref):
+def send_kernel(prompt_ref, q_ref, out_ref):
     wide = HALVES * NY * ROWS
-    mates = (col_ref[...] == row_ref[...]) & (
-        iota((ROWS, wide), 0) < iota((ROWS, wide), 1) % ROWS
-    )
-    rank = jnp.sum(mates.astype(jnp.int32), axis=0, keepdims=True)
-    slot = row_ref[...] * CAP + rank
+    lane = iota((1, wide), 1) % ROWS
+    slot = jnp.zeros((1, wide), jnp.int32)
+    for i in range(ROWS):
+        rank = sum((prompt_ref[j] == prompt_ref[i]).astype(jnp.int32) for j in range(i))
+        slot = jnp.where(lane == i, prompt_ref[i] * CAP + rank, slot)
     unit = NY * LINES
     rows = NX * unit
     r = iota((rows, wide), 0)
@@ -164,9 +164,13 @@
     return pl.pallas_call(
         send_kernel,
         out_shape=jax.ShapeDtypeStruct((ARR, PART), BF16),
-        compiler_params=pltpu.CompilerParams(vmem_limit_bytes=32 * MB),
+        in_specs=[
+            pl.BlockSpec(memory_space=pltpu.SMEM),
+            pl.BlockSpec(memory_space=pltpu.VMEM),
+        ],
+        compiler_params=pltpu.CompilerParams(vmem_limit_bytes=12 * MB),
         name="fill_sends",
-    )(prompt_ids, jnp.tile(prompt_ids.reshape(1, ROWS), (1, HALVES * NY)), queries)
+    )(prompt_ids[:, 0], queries)
 
 
 def suffix_kernel(table_ref, len_ref, q_ref, pool_ref, out_ref, lse_ref, kv, sems):
@@ -220,7 +224,7 @@
             pltpu.VMEM((ROWS, SPAN, 2 * KVW), BF16),
             pltpu.SemaphoreType.DMA((ROWS,)),
         ],
-        compiler_params=pltpu.CompilerParams(vmem_limit_bytes=48 * MB),
+        compiler_params=pltpu.CompilerParams(vmem_limit_bytes=20 * MB),
         cost_estimate=pl.CostEstimate(
             flops=10**9, bytes_accessed=9 * MB, transcendentals=0
         ),
@@ -267,7 +271,7 @@
             jax.ShapeDtypeStruct((2, GROUP, HALF, HD), BF16),
             jax.ShapeDtypeStruct((8, ARR), jnp.int32),
         ],
-        compiler_params=pltpu.CompilerParams(vmem_limit_bytes=24 * MB),
+        compiler_params=pltpu.CompilerParams(vmem_limit_bytes=16 * MB),
         name="gather_rows",
     )(arrived)
 
@@ -346,7 +350,7 @@
         ],
         in_specs=[vmem] * (2 + len(kv) + len(state)),
         out_specs=[vmem, vmem],
-        compiler_params=pltpu.CompilerParams(vmem_limit_bytes=32 * MB),
+        compiler_params=pltpu.CompilerParams(vmem_limit_bytes=16 * MB),
         cost_estimate=pl.CostEstimate(
             flops=blocks * 4 * 10**9, bytes_accessed=8 * MB, transcendentals=0
         ),
@@ -355,7 +359,7 @@
 
 
 def last_kernel(q_ref, place_ref, sum_ref, total_ref, *refs):
-    kv_refs, all_refs, (out_ref, os, ls, held, sems) = refs[:2], refs[2:10], refs[10:]
+    kv_refs, all_refs, (final_ref, os, ls, held, sems, out_ref, out_sems) = refs[:2], refs[2:10], refs[10:]
     for turn in range(2):
         os[turn] = jnp.zeros((GROUP // 2, HALF, 2 * HD), BF16)
         ls[turn] = jnp.zeros((HALF, HD), BF16)
@@ -421,13 +425,24 @@
         ],
         axis=1,
     )
+    copies = []
+
+    def send(p, width, piece):
+        cut = pl.ds(p * 2 * HD, width)
+        out_ref[:, cut] = piece.astype(BF16)
+        copy = pltpu.make_async_copy(out_ref.at[:, cut], final_ref.at[:, cut], out_sems.at[p])
+        copy.start()
+        copies.append(copy)
+
     for p in range(PAIRS):
         source = jnp.concatenate(
             [os[turn, half * PAIRS + p] for turn in range(2) for half in range(HALVES)], axis=0
         )
-        out_ref[:, p * 2 * HD : (p + 1) * 2 * HD] = dot(scatter, source).astype(BF16)
+        send(p, 2 * HD, dot(scatter, source))
     source = jnp.concatenate([ls[0], ls[0], ls[1], ls[1]], axis=0)
-    out_ref[:, PART:] = dot(scatter, source).astype(BF16)
+    send(PAIRS, HD, dot(scatter, source))
+    for copy in copies:
+        copy.wait()
 
 
 def finish_prefix(rows, place, state, last, everything):
@@ -436,13 +451,16 @@
         last_kernel,
         out_shape=jax.ShapeDtypeStruct((ARR, PART + HD), BF16),
         in_specs=[vmem] * 6 + [pl.BlockSpec(memory_space=pl.ANY)] * 8,
+        out_specs=pl.BlockSpec(memory_space=pltpu.HBM),
         scratch_shapes=[
             pltpu.VMEM((2, GROUP // 2, HALF, 2 * HD), BF16),
             pltpu.VMEM((2, HALF, HD), BF16),
             pltpu.VMEM((2, BLOCK, HD), BF16),
             pltpu.SemaphoreType.DMA((1,)),
-        ],
-        compiler_params=pltpu.CompilerParams(vmem_limit_bytes=36 * MB),
+            pltpu.VMEM((ARR, PART + HD), BF16),
+            pltpu.SemaphoreType.DMA((PAIRS + 1,)),
+        ],
+        compiler_params=pltpu.CompilerParams(vmem_limit_bytes=20 * MB),
         cost_estimate=pl.CostEstimate(
             flops=6 * 10**9, bytes_accessed=8 * MB, transcendentals=0
         ),
@@ -488,7 +506,7 @@
     return pl.pallas_call(
         merge_kernel,
         out_shape=jax.ShapeDtypeStruct((ROWS, KVH * WIDE), BF16),
-        compiler_params=pltpu.CompilerParams(vmem_limit_bytes=32 * MB),
+        compiler_params=pltpu.CompilerParams(vmem_limit_bytes=16 * MB),
         name="merge",
     )(at.reshape(-1, 1), back, so, sl)
 
@@ -513,7 +531,7 @@
         ]
     ).astype(jnp.int32)
     sends = fill_sends(prompt_ids, queries)
-    sends, prefix_kv = lax.optimization_barrier((sends, prefix_kv))
+    sends, heads = lax.optimization_barrier((sends, heads))
     arrived = exchange(sends)
     pieces = split_heads(heads, prefix_kv)
 
@@ -521,12 +539,10 @@
         return lax.ppermute(piece, AXES, routes(n // 2, n % 2))
 
     kv = list(pieces)
-    for n in (2, 3, 6, 7, 1):
+    for n in (1, 2, 3, 6, 7):
         kv[n] = move(n, pieces[n])
-    kv[1], later, queries = lax.optimization_barrier((kv[1], pieces[4], queries))
+    arrived, kv[1], later = lax.optimization_barrier((arrived, kv[1], pieces[4]))
     kv[4] = move(4, later)
-    so, sl = suffix(page_table, suffix_len, queries, suffix_pool)
-    arrived, so, sl = lax.optimization_barrier((arrived, so, sl))
     rows, place = gather_rows(arrived)
     state = add_sums(rows, place, kv[0:2], ())
     state, kv[2], kv[3], kv[6], kv[7], later = lax.optimization_barrier(
@@ -534,8 +550,10 @@
     )
     kv[5] = move(5, later)
     state = add_sums(rows, place, kv[2:4] + kv[6:8], state)
-    back = exchange(finish_prefix(rows, place, state, kv[4:6], kv))
-    return merge(prompt_ids, back, so, sl)
+    parts = finish_prefix(rows, place, state, kv[4:6], kv)
+    parts, queries = lax.optimization_barrier((parts, queries))
+    so, sl = suffix(page_table, suffix_len, queries, suffix_pool)
+    return merge(prompt_ids, exchange(parts), so, sl)
 
 
 def solution(mesh):

time: 164 us -> 164 us (level)
  Pallas kernels: 70.2 us -> 83.4 us
  starting transfers between devices: 53.1 us -> 46.7 us
  waiting for transfers between devices: 28.2 us -> 23.2 us
    pallas_call x1, Pallas kernels: 5.6 us -> 15.6 us  [suffix(): pl.pallas_call(suffix_kernel, out_shape=[shape, shape], in_specs=[smem, s...]
    all_to_all x2, waiting for transfers between devices: 27.7 us -> 18.9 us  [exchange(): lax.all_to_all(array.reshape(DEVS, LINES, width), AXES, split_axis=0, con...]
    ppermute x7, waiting for transfers between devices: 0.58 us -> 4.32 us  [move(): return lax.ppermute(piece, AXES, routes(n // 2, n % 2))]
    all_to_all x2, starting transfers between devices: 41.6 us -> 38 us  [exchange(): lax.all_to_all(array.reshape(DEVS, LINES, width), AXES, split_axis=0, con...]
    ppermute x7, starting transfers between devices: 11.5 us -> 8.67 us  [move(): return lax.ppermute(piece, AXES, routes(n // 2, n % 2))]
    pallas_call x1, Pallas kernels: 40.2 us -> 42.9 us  [finish_prefix(): pl.pallas_call(last_kernel, out_shape=jax.ShapeDtypeStruct((ARR, PART + H...]
    unnamed x29 -> x22, local copies, waits for them, and re-layouts: 7.54 us -> 9.2 us
  transfers between devices with their start and end apart: 9 -> 9, of which waited for: 4 -> 5; matrix products, arithmetic and copies ran while one was open for 2% -> 1% of each run, Pallas kernels for 16% -> 22%
where the time goes in v4:
time: 164 us
  Pallas kernels  83.4 us (51%)
  starting transfers between devices  46.7 us (28%)
  waiting for transfers between devices  23.2 us (14%)
  local copies, waits for them, and re-layouts  9.71 us (6%)
    pallas_call x1, Pallas kernels, finish_prefix(): pl.pallas_call(last_kernel, out_shape=jax.ShapeDtypeStruct((ARR, PART + H...  42.9 us
    all_to_all x2, starting transfers between devices, exchange(): lax.all_to_all(array.reshape(DEVS, LINES, width), AXES, split_axis=0, con...  38 us
    all_to_all x2, waiting for transfers between devices, exchange(): lax.all_to_all(array.reshape(DEVS, LINES, width), AXES, split_axis=0, con...  18.9 us
    pallas_call x1, Pallas kernels, suffix(): pl.pallas_call(suffix_kernel, out_shape=[shape, shape], in_specs=[smem, s...  15.6 us
    pallas_call x2, Pallas kernels, add_sums(): pl.pallas_call(functools.partial(sums_kernel, blocks, not state), out_sha...  14.8 us
    unnamed x22, local copies, waits for them, and re-layouts  9.2 us
    ppermute x7, starting transfers between devices, move(): return lax.ppermute(piece, AXES, routes(n // 2, n % 2))  8.67 us
    ppermute x7, waiting for transfers between devices, move(): return lax.ppermute(piece, AXES, routes(n // 2, n % 2))  4.32 us
  transfers between devices with their start and end apart: 9, of which 5 were waited for; matrix products, arithmetic and copies ran while one was open for 1% of the time, Pallas kernels for 22%

profile of v4, /device:TPU:0, one launch (start us, length us, event | category | flops | bytes accessed | tf_op | source)
XLA Modules:
  0.0 163.7 jit_solution(14822938782144201929)
XLA Ops:
  0.0 0.9 copy-done.3
  0.9 0.7 copy-done.6
  1.6 2.1 %fill_sends.1 = bf16[1024,768]{1,0:T(8,128)(2,1)} custom-call(s32[8]{0:T(128)S(1)} %bitcast.26, bf16[8,12288]{1,0:T(8,128)(2,1)S(1)} %copy-done.3), custom_call_target="tpu_custom_call" | custom-call | tf_op jit(solution)/shard_map/fill_sends/pallas_call | solution.py:164
  3.7 0.1 stack.35.head_ref
  3.8 11.1 %all-to-all-start = ((bf16[128,8,768]{2,1,0:T(8,128)(2,1)}), bf16[128,8,768]{2,1,0:T(8,128)(2,1)S(1)}, u32[]{:S(2)}, u32[]{:S(2)}) async-start(bf16[128,8,768]{2,1,0:T(8,128)(2,1)} %bitcast.9), calls=%async_computation | async-start | bytes 3145728 | tf_op jit(solution)/shard_map/all_to_all | solution.py:516
  15.0 2.2 %copy-done.1 = bf16[1,1024,2048]{2,1,0:T(8,128)(2,1)S(1)} copy-done((bf16[1,1024,2048]{2,1,0:T(8,128)(2,1)S(1)}, bf16[1,1024,2048]{2,1,0:T(8,128)(2,1)}, u32[]{:S(2)}) %copy-start.1) | copy-done | bytes 4194328
  17.2 3.3 %split_heads.1 = (bf16[2,1024,128]{2,1,0:T(8,128)(2,1)S(1)}, bf16[2,1024,128]{2,1,0:T(8,128)(2,1)S(1)}, bf16[2,1024,128]{2,1,0:T(8,128)(2,1)}, bf16[2,1024,128]{...) custom-call(s32[8]{0:T(128)S(1)} %stack.35.head_ref, ...), custom_call_target="tpu_custom_call" | custom-call | tf_op jit(solution)/shard_map/split_heads/pallas_call | solution.py:100
  20.5 0.8 copy-done.9
  21.3 1.2 collective-permute-start.1
  22.5 1.0 collective-permute-start.2
  23.6 3.5 %collective-permute-start.3 = (bf16[2,1024,128]{2,1,0:T(8,128)(2,1)}, bf16[2,1024,128]{2,1,0:T(8,128)(2,1)}, u32[]{:S(2)}, u32[]{:S(2)}) collective-permute-start(bf16[2,1024,128]{2,1,0:T(8,128)(2,1)} %get-tuple-element.48), channel_id=1, source_target_pairs={{0,12},{1,13},{2,14},{3,15},{4,0},{5,1},{6,2},{7,3},{8,4},{9,5},{1... | collective-permute-start | bytes 1572872 | tf_op jit(solution)/shard_map/ppermute | solution.py:539
  27.0 0.3 collective-permute-start.4
  27.4 12.1 %all-to-all-done = bf16[128,8,768]{2,1,0:T(8,128)(2,1)S(1)} async-done(((bf16[128,8,768]{2,1,0:T(8,128)(2,1)}), bf16[128,8,768]{2,1,0:T(8,128)(2,1)S(1)}, u32[]{:S(2)}, u32[]{:S(2)}) %all-to-all-start) | async-done | bytes 1572896 | tf_op jit(solution)/shard_map/all_to_all | solution.py:516
  39.4 2.4 %gather_rows.1 = (bf16[2,12,256,128]{3,2,1,0:T(8,128)(2,1)S(1)}, s32[8,1024]{1,0:T(8,128)S(1)}) custom-call(bf16[1024,768]{1,0:T(8,128)(2,1)S(1)} %bitcast.22), custom_call_target="tpu_custom_call" | custom-call | tf_op jit(solution)/shard_map/gather_rows/pallas_call | solution.py:268
  41.9 5.3 %sums_1.1 = (f32[2,12,256,128]{3,2,1,0:T(8,128)S(1)}, f32[2,256,128]{2,1,0:T(8,128)S(1)}) custom-call(bf16[2,12,256,128]{3,2,1,0:T(8,128)(2,1)S(1)} %get-tuple-element.40.q_ref, s32[8,1024]{1,0:T(8,128)S(1)} %get-tuple-element.41.place_ref, bf16[2,1024,128]{2,1,0:T(8,128)(2,1)S(1)} %get-tuple-element.42.refs_0_.refs_2_, ...), custom_call_target="tpu_custom_call" | custom-call | flops 4000000000 | bytes 8388608 | tf_op jit(solution)/shard_map/sums_1/pallas_call | solution.py:345
  47.2 0.6 collective-permute-done.1.refs_0_.refs_4_
  47.8 0.4 collective-permute-start.6
  48.2 2.2 %collective-permute-start.5 = (bf16[2,1024,128]{2,1,0:T(8,128)(2,1)S(1)}, bf16[2,1024,128]{2,1,0:T(8,128)(2,1)S(1)}, u32[]{:S(2)}, u32[]{:S(2)}) collective-permute-start(bf16[2,1024,128]{2,1,0:T(8,128)(2,1)S(1)} %get-tuple-element.59), channel_id=1, source_target_pairs={{0,8},{1,9},{2,10},{3,11},{4,12},{5,13},{6,14},{7,15},{8,0},{9,1},... | collective-permute-start | bytes 1572872 | tf_op jit(solution)/shard_map/ppermute | solution.py:539
  50.4 9.4 %sums_2.1 = (f32[2,12,256,128]{3,2,1,0:T(8,128)S(1)}, f32[2,256,128]{2,1,0:T(8,128)S(1)}) custom-call(bf16[2,12,256,128]{3,2,1,0:T(8,128)(2,1)S(1)} %get-tuple-element.40.q_ref, s32[8,1024]{1,0:T(8,128)S(1)} %get-tuple-element.41.place_ref, bf16[2,1024,128]{2,1,0:T(8,128)(2,1)} %collective-permute-done.1.refs_0_.refs_4_, ...), custom_call_target="tpu_custom_call" | custom-call | flops 8000000000 | bytes 8388608 | tf_op jit(solution)/shard_map/sums_2/pallas_call | solution.py:345
  59.9 2.9 %collective-permute-done.6.refs_1_.refs_7_ = bf16[2,1024,128]{2,1,0:T(8,128)(2,1)S(1)} collective-permute-done((bf16[2,1024,128]{2,1,0:T(8,128)(2,1)S(1)}, bf16[2,1024,128]{2,1,0:T(8,128)(2,1)S(1)}, u32[]{:S(2)}, u32[]{:S(2)}) %collective-permute-start.6) | collective-permute-done | bytes 524320 | tf_op jit(solution)/shard_map/ppermute | solution.py:539
  62.8 0.8 collective-permute-done.5.refs_0_.refs_6_
  63.6 42.9 %finish_prefix.1 = bf16[1024,896]{1,0:T(8,128)(2,1)S(1)} custom-call(bf16[2,12,256,128]{3,2,1,0:T(8,128)(2,1)S(1)} %get-tuple-element.40.q_ref, s32[8,1024]{1,0:T(8,128)S(1)} %get-tuple-element.41.place_ref, f32[2,12,256,128]{3,2,1,0:T(8,128)S(1)} %get-tuple-element.57.sum_ref, f32[2,256,128]{2,1,0:T(8,128)S(1)} %get-tuple-element.58.total_ref, ...), custom_call_target="tpu_custom_call" | custom-call | flops 6000000000 | bytes 8388608 | tf_op jit(solution)/shard_map/finish_prefix/pallas_call | solution.py:450
  106.6 1.2 copy-done.2
  107.8 26.9 %all-to-all-start.1 = ((bf16[128,8,896]{2,1,0:T(8,128)(2,1)}), bf16[128,8,896]{2,1,0:T(8,128)(2,1)S(1)}, u32[]{:S(2)}, u32[]{:S(2)}) async-start(bf16[128,8,896]{2,1,0:T(8,128)(2,1)} %bitcast.23), calls=%async_computation.1 | async-start | bytes 3670016 | tf_op jit(solution)/shard_map/all_to_all | solution.py:516
  134.7 0.2 convert_reduce_fusion
  135.0 0.1 multiply_add_fusion
  135.1 0.1 reshape.329.at_ref
  135.3 0.2 reshape.325
  135.5 3.4 %copy-done = bf16[128,16,2048]{2,1,0:T(8,128)(2,1)S(1)} copy-done((bf16[128,16,2048]{2,1,0:T(8,128)(2,1)S(1)}, bf16[128,16,2048]{2,1,0:T(8,128)(2,1)}, u32[]{:S(2)}) %copy-start) | copy-done | bytes 8388632
  138.9 15.6 %suffix.1 = (f32[8,8,16,128]{3,2,1,0:T(8,128)S(1)}, f32[8,8,16,128]{3,2,1,0:T(8,128)S(1)}) custom-call(s32[8,16]{1,0:T(8,128)S(1)} %copy-done.5, s32[8]{0:T(128)S(1)} %copy-done.8, bf16[8,8,16,128]{3,2,1,0:T(8,128)(2,1)S(1)} %pad.4.q_ref, bf16[128,16,2048]{2,1,0:T(8,128)(2,1)S(1)} %copy-done), custom_call_target="tpu_custom_call" | custom-call | flops 1000000000 | bytes 9437184 | tf_op jit(solution)/shard_map/suffix/pallas_call | solution.py:218
  154.6 6.8 %all-to-all-done.1 = bf16[128,8,896]{2,1,0:T(8,128)(2,1)S(1)} async-done(((bf16[128,8,896]{2,1,0:T(8,128)(2,1)}), bf16[128,8,896]{2,1,0:T(8,128)(2,1)S(1)}, u32[]{:S(2)}, u32[]{:S(2)}) %all-to-all-start.1) | async-done | bytes 1835040 | tf_op jit(solution)/shard_map/all_to_all | solution.py:516
  161.5 2.2 %merge.1 = bf16[8,12288]{1,0:T(8,128)(2,1)} custom-call(s32[256,1]{1,0:T(8,128)S(1)} %reshape.329.at_ref, bf16[1024,896]{1,0:T(8,128)(2,1)S(1)} %bitcast.21, f32[8,12288]{1,0:T(8,128)S(1)} %reshape.326.so_ref, f32[8,12288]{1,0:T(8,128)S(1)} %reshape.327.sl_ref), custom_call_target="tpu_custom_call" | custom-call | tf_op jit(solution)/shard_map/merge/pallas_call | solution.py:506
  (29 shorter events, 0.4 us)
Async XLA Ops:
  0.0 0.9 copy-start.3
  0.9 0.7 copy-start.6
  3.8 35.6 %all-to-all-start = ((bf16[128,8,768]{2,1,0:T(8,128)(2,1)}), bf16[128,8,768]{2,1,0:T(8,128)(2,1)S(1)}, u32[]{:S(2)}, u32[]{:S(2)}) async-start(bf16[128,8,768]{2,1,0:T(8,128)(2,1)} %bitcast.9), calls=%async_computation | async-start | bytes 3145728 | tf_op jit(solution)/shard_map/all_to_all | solution.py:516
  15.0 2.2 %copy-start.1 = (bf16[1,1024,2048]{2,1,0:T(8,128)(2,1)S(1)}, bf16[1,1024,2048]{2,1,0:T(8,128)(2,1)}, u32[]{:S(2)}) copy-start(bf16[1,1024,2048]{2,1,0:T(8,128)(2,1)} %kv_ref.1) | copy-start | bytes 12582916
  20.5 0.8 copy-start.9
  21.3 6.1 %collective-permute-start = (bf16[2,1024,128]{2,1,0:T(8,128)(2,1)S(1)}, bf16[2,1024,128]{2,1,0:T(8,128)(2,1)S(1)}, u32[]{:S(2)}, u32[]{:S(2)}) collective-permute-start(bf16[2,1024,128]{2,1,0:T(8,128)(2,1)S(1)} %get-tuple-element.37), channel_id=1, source_target_pairs={{0,16},{1,17},{2,18},{3,19},{4,20},{5,21},{6,22},{7,23},{8,24},{9,... | collective-permute-start | bytes 1572872 | tf_op jit(solution)/shard_map/ppermute | solution.py:539
  21.3 26.5 %collective-permute-start.1 = (bf16[2,1024,128]{2,1,0:T(8,128)(2,1)}, bf16[2,1024,128]{2,1,0:T(8,128)(2,1)}, u32[]{:S(2)}, u32[]{:S(2)}) collective-permute-start(bf16[2,1024,128]{2,1,0:T(8,128)(2,1)} %get-tuple-element.46), channel_id=1, source_target_pairs={{0,4},{1,5},{2,6},{3,7},{4,8},{5,9},{6,10},{7,11},{8,12},{9,13},{1... | collective-permute-start | bytes 1572872 | tf_op jit(solution)/shard_map/ppermute | solution.py:539
  22.5 25.2 %collective-permute-start.2 = (bf16[2,1024,128]{2,1,0:T(8,128)(2,1)}, bf16[2,1024,128]{2,1,0:T(8,128)(2,1)}, u32[]{:S(2)}, u32[]{:S(2)}) collective-permute-start(bf16[2,1024,128]{2,1,0:T(8,128)(2,1)} %get-tuple-element.47), channel_id=1, source_target_pairs={{0,17},{1,18},{2,19},{3,16},{4,21},{5,22},{6,23},{7,20},{8,25},{9,... | collective-permute-start | bytes 1572872 | tf_op jit(solution)/shard_map/ppermute | solution.py:539
  23.6 24.2 %collective-permute-start.3 = (bf16[2,1024,128]{2,1,0:T(8,128)(2,1)}, bf16[2,1024,128]{2,1,0:T(8,128)(2,1)}, u32[]{:S(2)}, u32[]{:S(2)}) collective-permute-start(bf16[2,1024,128]{2,1,0:T(8,128)(2,1)} %get-tuple-element.48), channel_id=1, source_target_pairs={{0,12},{1,13},{2,14},{3,15},{4,0},{5,1},{6,2},{7,3},{8,4},{9,5},{1... | collective-permute-start | bytes 1572872 | tf_op jit(solution)/shard_map/ppermute | solution.py:539
  27.0 20.8 %collective-permute-start.4 = (bf16[2,1024,128]{2,1,0:T(8,128)(2,1)}, bf16[2,1024,128]{2,1,0:T(8,128)(2,1)}, u32[]{:S(2)}, u32[]{:S(2)}) collective-permute-start(bf16[2,1024,128]{2,1,0:T(8,128)(2,1)} %get-tuple-element.49), channel_id=1, source_target_pairs={{0,19},{1,16},{2,17},{3,18},{4,23},{5,20},{6,21},{7,22},{8,27},{9,... | collective-permute-start | bytes 1572872 | tf_op jit(solution)/shard_map/ppermute | solution.py:539
  41.9 5.9 %copy-start.10 = (bf16[2,1024,128]{2,1,0:T(8,128)(2,1)S(1)}, bf16[2,1024,128]{2,1,0:T(8,128)(2,1)}, u32[]{:S(2)}) copy-start(bf16[2,1024,128]{2,1,0:T(8,128)(2,1)} %copy-done.9) | copy-start | bytes 1572868
  47.8 14.9 %collective-permute-start.6 = (bf16[2,1024,128]{2,1,0:T(8,128)(2,1)S(1)}, bf16[2,1024,128]{2,1,0:T(8,128)(2,1)S(1)}, u32[]{:S(2)}, u32[]{:S(2)}) collective-permute-start(bf16[2,1024,128]{2,1,0:T(8,128)(2,1)S(1)} %copy-done.10), channel_id=1, source_target_pairs={{0,18},{1,19},{2,16},{3,17},{4,22},{5,23},{6,20},{7,21},{8,26},{9,... | collective-permute-start | bytes 1572872 | tf_op jit(solution)/shard_map/ppermute | solution.py:539
  48.2 15.4 %collective-permute-start.5 = (bf16[2,1024,128]{2,1,0:T(8,128)(2,1)S(1)}, bf16[2,1024,128]{2,1,0:T(8,128)(2,1)S(1)}, u32[]{:S(2)}, u32[]{:S(2)}) collective-permute-start(bf16[2,1024,128]{2,1,0:T(8,128)(2,1)S(1)} %get-tuple-element.59), channel_id=1, source_target_pairs={{0,8},{1,9},{2,10},{3,11},{4,12},{5,13},{6,14},{7,15},{8,0},{9,1},... | collective-permute-start | bytes 1572872 | tf_op jit(solution)/shard_map/ppermute | solution.py:539
  106.5 1.3 copy-start.2
  107.8 26.9 %copy-start.7 = (s32[8,1]{0,1:T(1,128)S(1)}, s32[8,1]{0,1:T(1,128)}, u32[]{:S(2)}) copy-start(s32[8,1]{0,1:T(1,128)} %param.7) | copy-start | bytes 100
  107.8 27.4 %copy-start.4 = (bf16[8,12288]{1,0:T(8,128)(2,1)S(1)}, bf16[8,12288]{1,0:T(8,128)(2,1)}, u32[]{:S(2)}) copy-start(bf16[8,12288]{1,0:T(8,128)(2,1)} %q_ref.1) | copy-start | bytes 589828
  107.8 27.7 %copy-start.5 = (s32[8,16]{1,0:T(8,128)S(1)}, s32[8,16]{1,0:T(8,128)}, u32[]{:S(2)}) copy-start(s32[8,16]{1,0:T(8,128)} %table_ref.1) | copy-start | bytes 1540
  107.8 27.7 %copy-start.8 = (s32[8]{0:T(128)S(1)}, s32[8]{0:T(128)}, u32[]{:S(2)}) copy-start(s32[8]{0:T(128)} %len_ref.1) | copy-start | bytes 100
  107.8 53.7 %all-to-all-start.1 = ((bf16[128,8,896]{2,1,0:T(8,128)(2,1)}), bf16[128,8,896]{2,1,0:T(8,128)(2,1)S(1)}, u32[]{:S(2)}, u32[]{:S(2)}) async-start(bf16[128,8,896]{2,1,0:T(8,128)(2,1)} %bitcast.23), calls=%async_computation.1 | async-start | bytes 3670016 | tf_op jit(solution)/shard_map/all_to_all | solution.py:516
  135.5 3.4 %copy-start = (bf16[128,16,2048]{2,1,0:T(8,128)(2,1)S(1)}, bf16[128,16,2048]{2,1,0:T(8,128)(2,1)}, u32[]{:S(2)}) copy-start(bf16[128,16,2048]{2,1,0:T(8,128)(2,1)} %pool_ref.1) | copy-start | bytes 25165828

commit v5 on v4

--- a/solution.py
+++ b/solution.py
@@ -58,24 +58,27 @@
     return ((x * NC + c) * NZ + z) * NY + y
 
 
-def routes(k, cross):
+def routes(step):
     pairs = []
     for x in range(NX):
         for c in range(NC):
             for z in range(NZ):
                 for y in range(NY):
-                    if (c ^ cross) == 0:
-                        to = device_number(x, 0, (z + k) % NZ, y)
+                    if step is None:
+                        to = device_number(x, 1 - c, z, y)
+                    elif c == 0:
+                        to = device_number(x, 0, (z + step) % NZ, y)
                     else:
-                        to = device_number(x, 1, z, (y + k) % NY)
+                        to = device_number(x, 1, z, (y + step) % NY)
                     pairs.append((device_number(x, c, z, y), to))
     return pairs
 
 
 def split_heads_kernel(head_ref, kv_ref, *refs):
     outs, (held, sems) = refs[:-2], refs[-2:]
+    places = [out for out in outs[:4]] + [outs[4].at[k] for k in range(4)]
     inward, outward = [], []
-    for i, out in enumerate(outs):
+    for i, out in enumerate(places):
         for part in range(2):
             start = pl.multiple_of(part * KVW + head_ref[i] * HD, HD)
             inward.append(
@@ -86,6 +89,7 @@
             outward.append(
                 pltpu.make_async_copy(held.at[i, part], out.at[part], sems.at[1, i, part])
             )
+    inward, outward = inward[8:] + inward[:8], outward[8:] + outward[:8]
     for copy in inward:
         copy.start()
     for copy, onward in zip(inward, outward):
@@ -97,18 +101,36 @@
 
 def split_heads(heads, prefix_kv):
     n = heads.shape[0]
+    any_place = pl.BlockSpec(memory_space=pl.ANY)
     return pl.pallas_call(
         split_heads_kernel,
-        out_shape=[jax.ShapeDtypeStruct((2, BLOCK, HD), BF16)] * n,
-        in_specs=[pl.BlockSpec(memory_space=pltpu.SMEM), pl.BlockSpec(memory_space=pltpu.HBM)],
-        out_specs=[pl.BlockSpec(memory_space=pltpu.HBM)] * n,
+        out_shape=[jax.ShapeDtypeStruct((2, BLOCK, HD), BF16)] * 4
+        + [jax.ShapeDtypeStruct((4, 2, BLOCK, HD), BF16)],
+        in_specs=[pl.BlockSpec(memory_space=pltpu.SMEM), any_place],
+        out_specs=[any_place] * 5,
         scratch_shapes=[
             pltpu.VMEM((n, 2, BLOCK, HD), BF16),
             pltpu.SemaphoreType.DMA((2, n, 2)),
         ],
-        compiler_params=pltpu.CompilerParams(vmem_limit_bytes=8 * MB),
+        compiler_params=pltpu.CompilerParams(vmem_limit_bytes=60 * MB),
         name="split_heads",
     )(heads, prefix_kv)
+
+
+def pair_kernel(*refs):
+    other_ref = refs[4]
+    for k in range(4):
+        refs[5 + k][0] = refs[k][...]
+        refs[5 + k][1] = other_ref[k]
+
+
+def pair_up(own, other):
+    return pl.pallas_call(
+        pair_kernel,
+        out_shape=[jax.ShapeDtypeStruct((2, 2, BLOCK, HD), BF16)] * 4,
+        compiler_params=pltpu.CompilerParams(vmem_limit_bytes=20 * MB),
+        name="pair_up",
+    )(*own, other)
 
 
 def send_kernel(prompt_ref, q_ref, out_ref):
@@ -224,7 +246,7 @@
             pltpu.VMEM((ROWS, SPAN, 2 * KVW), BF16),
             pltpu.SemaphoreType.DMA((ROWS,)),
         ],
-        compiler_params=pltpu.CompilerParams(vmem_limit_bytes=20 * MB),
+        compiler_params=pltpu.CompilerParams(vmem_limit_bytes=56 * MB),
         cost_estimate=pl.CostEstimate(
             flops=10**9, bytes_accessed=9 * MB, transcendentals=0
         ),
@@ -309,9 +331,8 @@
 
 def tile_part(q_ref, kv_refs, turn, at):
     q = q_ref[turn, :, pl.ds(at, TILE), :].reshape(GROUP * TILE, HD)
-    mine = kv_refs[turn::2]
-    keys = jnp.concatenate([ref[0] for ref in mine], axis=0)
-    values = jnp.concatenate([ref[1] for ref in mine], axis=0)
+    keys = jnp.concatenate([ref[turn, 0] for ref in kv_refs], axis=0)
+    values = jnp.concatenate([ref[turn, 1] for ref in kv_refs], axis=0)
     return plain_part(q, keys, values)
 
 
@@ -324,7 +345,7 @@
 
 
 def sums_kernel(blocks, first, q_ref, place_ref, *refs):
-    kv_refs, refs = refs[: 2 * blocks], refs[2 * blocks :]
+    kv_refs, refs = refs[:blocks], refs[blocks:]
     out_ref, total_ref = refs[-2:]
     for turn, count in enumerate(row_counts(place_ref)):
 
@@ -340,7 +361,7 @@
 
 
 def add_sums(rows, place, kv, state):
-    blocks = len(kv) // 2
+    blocks = len(kv)
     vmem = pl.BlockSpec(memory_space=pltpu.VMEM)
     return pl.pallas_call(
         functools.partial(sums_kernel, blocks, not state),
@@ -359,7 +380,7 @@
 
 
 def last_kernel(q_ref, place_ref, sum_ref, total_ref, *refs):
-    kv_refs, all_refs, (final_ref, os, ls, held, sems, out_ref, out_sems) = refs[:2], refs[2:10], refs[10:]
+    kv_refs, all_refs, (out_ref, os, ls, held, sems) = refs[:1], refs[1:5], refs[5:]
     for turn in range(2):
         os[turn] = jnp.zeros((GROUP // 2, HALF, 2 * HD), BF16)
         ls[turn] = jnp.zeros((HALF, HD), BF16)
@@ -392,7 +413,7 @@
                 q = q_ref[turn, :, pl.ds(at, TILE), :].reshape(GROUP * TILE, HD)
                 top = amount = acc = None
                 for k in range(4):
-                    copy = pltpu.make_async_copy(all_refs[k * 2 + turn], held, sems.at[0])
+                    copy = pltpu.make_async_copy(all_refs[k].at[turn], held, sems.at[0])
                     copy.start()
                     copy.wait()
                     score = dot_t(q, held[0])
@@ -425,24 +446,13 @@
         ],
         axis=1,
     )
-    copies = []
-
-    def send(p, width, piece):
-        cut = pl.ds(p * 2 * HD, width)
-        out_ref[:, cut] = piece.astype(BF16)
-        copy = pltpu.make_async_copy(out_ref.at[:, cut], final_ref.at[:, cut], out_sems.at[p])
-        copy.start()
-        copies.append(copy)
-
     for p in range(PAIRS):
         source = jnp.concatenate(
             [os[turn, half * PAIRS + p] for turn in range(2) for half in range(HALVES)], axis=0
         )
-        send(p, 2 * HD, dot(scatter, source))
+        out_ref[:, p * 2 * HD : (p + 1) * 2 * HD] = dot(scatter, source).astype(BF16)
     source = jnp.concatenate([ls[0], ls[0], ls[1], ls[1]], axis=0)
-    send(PAIRS, HD, dot(scatter, source))
-    for copy in copies:
-        copy.wait()
+    out_ref[:, PART:] = dot(scatter, source).astype(BF16)
 
 
 def finish_prefix(rows, place, state, last, everything):
@@ -450,17 +460,14 @@
     return pl.pallas_call(
         last_kernel,
         out_shape=jax.ShapeDtypeStruct((ARR, PART + HD), BF16),
-        in_specs=[vmem] * 6 + [pl.BlockSpec(memory_space=pl.ANY)] * 8,
-        out_specs=pl.BlockSpec(memory_space=pltpu.HBM),
+        in_specs=[vmem] * 5 + [pl.BlockSpec(memory_space=pl.ANY)] * 4,
         scratch_shapes=[
             pltpu.VMEM((2, GROUP // 2, HALF, 2 * HD), BF16),
             pltpu.VMEM((2, HALF, HD), BF16),
             pltpu.VMEM((2, BLOCK, HD), BF16),
             pltpu.SemaphoreType.DMA((1,)),
-            pltpu.VMEM((ARR, PART + HD), BF16),
-            pltpu.SemaphoreType.DMA((PAIRS + 1,)),
-        ],
-        compiler_params=pltpu.CompilerParams(vmem_limit_bytes=20 * MB),
+        ],
+        compiler_params=pltpu.CompilerParams(vmem_limit_bytes=36 * MB),
         cost_estimate=pl.CostEstimate(
             flops=6 * 10**9, bytes_accessed=8 * MB, transcendentals=0
         ),
@@ -526,31 +533,26 @@
     heads = jnp.stack(
         [
             jnp.where(c ^ cross == 0, (z + k) % NZ, NZ + (y + k) % NY)
+            for cross in range(2)
             for k in range(4)
-            for cross in range(2)
         ]
     ).astype(jnp.int32)
     sends = fill_sends(prompt_ids, queries)
     sends, heads = lax.optimization_barrier((sends, heads))
     arrived = exchange(sends)
-    pieces = split_heads(heads, prefix_kv)
-
-    def move(n, piece):
-        return lax.ppermute(piece, AXES, routes(n // 2, n % 2))
-
-    kv = list(pieces)
-    for n in (1, 2, 3, 6, 7):
-        kv[n] = move(n, pieces[n])
-    arrived, kv[1], later = lax.optimization_barrier((arrived, kv[1], pieces[4]))
-    kv[4] = move(4, later)
+    *own, other = split_heads(heads, prefix_kv)
+    other = lax.ppermute(other, AXES, routes(None))
+    pairs = pair_up(own, other)
+    arrived, first = lax.optimization_barrier((arrived, pairs[0]))
+    kv = [first] + [None] * 3
+    kv[1] = lax.ppermute(pairs[1], AXES, routes(1))
+    kv[3] = lax.ppermute(pairs[3], AXES, routes(3))
     rows, place = gather_rows(arrived)
-    state = add_sums(rows, place, kv[0:2], ())
-    state, kv[2], kv[3], kv[6], kv[7], later = lax.optimization_barrier(
-        (state, kv[2], kv[3], kv[6], kv[7], pieces[5])
-    )
-    kv[5] = move(5, later)
-    state = add_sums(rows, place, kv[2:4] + kv[6:8], state)
-    parts = finish_prefix(rows, place, state, kv[4:6], kv)
+    place, late = lax.optimization_barrier((place, pairs[2]))
+    kv[2] = lax.ppermute(late, AXES, routes(2))
+    state = add_sums(rows, place, kv[0:1], ())
+    state = add_sums(rows, place, [kv[1], kv[3]], state)
+    parts = finish_prefix(rows, place, state, kv[2:3], kv)
     parts, queries = lax.optimization_barrier((parts, queries))
     so, sl = suffix(page_table, suffix_len, queries, suffix_pool)
     return merge(prompt_ids, exchange(parts), so, sl)

time: 164 us -> 170 us (1.037)
  Pallas kernels: 83.4 us -> 74.1 us
  waiting for transfers between devices: 23.2 us -> 31.3 us
  starting transfers between devices: 46.7 us -> 51.9 us
    all_to_all x2, waiting for transfers between devices: 18.9 us -> 31.3 us  [exchange(): lax.all_to_all(array.reshape(DEVS, LINES, width), AXES, split_axis=0, con...]
    all_to_all x2, starting transfers between devices: 38 us -> 47.2 us  [exchange(): lax.all_to_all(array.reshape(DEVS, LINES, width), AXES, split_axis=0, con...]
    pallas_call x1, Pallas kernels: 15.6 us -> 6.95 us  [suffix(): pl.pallas_call(suffix_kernel, out_shape=[shape, shape], in_specs=[smem, s...]
    pallas_call x1, Pallas kernels: 42.9 us -> 38 us  [finish_prefix(): pl.pallas_call(last_kernel, out_shape=jax.ShapeDtypeStruct((ARR, PART + H...]
    ppermute x7 -> x4, waiting for transfers between devices: 4.32 us -> 0.05 us  [the longest x1 0.05 us: body(): kv[2] = lax.ppermute(late, AXES, routes(2))]
    ppermute x7 -> x4, starting transfers between devices: 8.67 us -> 4.69 us  [the longest x1 2.16 us: body(): kv[3] = lax.ppermute(pairs[3], AXES, routes(3))]
    pallas_call x0 -> x1, Pallas kernels: none -> 2.99 us  [pair_up(): pl.pallas_call(pair_kernel, out_shape=[jax.ShapeDtypeStruct((2, 2, BLOCK,...]
    unnamed x22 -> x26, local copies, waits for them, and re-layouts: 9.2 us -> 7.11 us
  transfers between devices with their start and end apart: 9 -> 6, of which waited for: 5 -> 2; matrix products, arithmetic and copies ran while one was open for 1% -> 2% of each run, Pallas kernels for 22% -> 16%
where the time goes in v5:
time: 170 us; the launch traced here: 169 us
  Pallas kernels  74.1 us (44%)
  starting transfers between devices  51.9 us (31%)
  waiting for transfers between devices  31.3 us (18%)
  local copies, waits for them, and re-layouts  11 us (6%)
    all_to_all x2, starting transfers between devices, exchange(): lax.all_to_all(array.reshape(DEVS, LINES, width), AXES, split_axis=0, con...  47.2 us
    pallas_call x1, Pallas kernels, finish_prefix(): pl.pallas_call(last_kernel, out_shape=jax.ShapeDtypeStruct((ARR, PART + H...  38 us
    all_to_all x2, waiting for transfers between devices, exchange(): lax.all_to_all(array.reshape(DEVS, LINES, width), AXES, split_axis=0, con...  31.3 us
    pallas_call x2, Pallas kernels, add_sums(): pl.pallas_call(functools.partial(sums_kernel, blocks, not state), out_sha...  14.4 us
    unnamed x26, local copies, waits for them, and re-layouts  7.11 us
    pallas_call x1, Pallas kernels, suffix(): pl.pallas_call(suffix_kernel, out_shape=[shape, shape], in_specs=[smem, s...  6.95 us
    pallas_call x1, Pallas kernels, split_heads(): pl.pallas_call(split_heads_kernel, out_shape=[jax.ShapeDtypeStruct((2, BL...  4.97 us
  transfers between devices with their start and end apart: 6, of which 2 were waited for; matrix products, arithmetic and copies ran while one was open for 2% of the time, Pallas kernels for 16%

profile of v5, /device:TPU:0, one launch (start us, length us, event | category | flops | bytes accessed | tf_op | source)
XLA Modules:
  0.0 169.0 jit_solution(5174279156194144902)
XLA Ops:
  0.0 0.9 copy-done.1
  0.9 0.7 copy-done.7
  1.6 2.1 %fill_sends.1 = bf16[1024,768]{1,0:T(8,128)(2,1)} custom-call(s32[8]{0:T(128)S(1)} %bitcast.24, bf16[8,12288]{1,0:T(8,128)(2,1)S(1)} %copy-done.1), custom_call_target="tpu_custom_call" | custom-call | tf_op jit(solution)/shard_map/fill_sends/pallas_call | solution.py:186
  3.7 0.7 stack.35.head_ref
  4.4 5.0 %split_heads.1 = (bf16[2,1024,128]{2,1,0:T(8,128)(2,1)}, bf16[2,1024,128]{2,1,0:T(8,128)(2,1)}, bf16[2,1024,128]{2,1,0:T(8,128)(2,1)}, bf16[2,1024,128]{2,1,0:T(8,128)(2,1)}, bf16[4,2,1024,128]{3,2,1,0:T(8,128)(2,1)}) custom-call(s32[8]{0:T(128)} %stack.35.head_ref, bf16[1,1024,2048]{2,1,0:T(8,128)(2,1)} %kv_ref.1), custom_call_target="tpu_custom_call" | custom-call | tf_op jit(solution)/shard_map/split_heads/pallas_call | solution.py:105
  9.4 0.1 collective-permute-start
  9.5 11.2 %all-to-all-start = ((bf16[128,8,768]{2,1,0:T(8,128)(2,1)}), bf16[128,8,768]{2,1,0:T(8,128)(2,1)S(1)}, u32[]{:S(2)}, u32[]{:S(2)}) async-start(bf16[128,8,768]{2,1,0:T(8,128)(2,1)} %bitcast.9), calls=%async_computation | async-start | bytes 3145728 | tf_op jit(solution)/shard_map/all_to_all | solution.py:523
  20.8 1.0 copy-done.6
  21.8 3.0 %pair_up.1 = (bf16[2,2,1024,128]{3,2,1,0:T(8,128)(2,1)S(1)}, bf16[2,2,1024,128]{3,2,1,0:T(8,128)(2,1)}, bf16[2,2,1024,128]{3,2,1,0:T(8,128)(2,1)S(1)}, bf16[2,2,1024,128]{3,2,1,0:T(8,128)(2,1)}) custom-call(bf16[2,1024,128]{2,1,0:T(8,128)(2,1)S(1)} %copy-done.3, bf16[2,1024,128]{2,1,0:T(8,128)(2,1)S(1)} %copy-done.4, bf16[2,1024,128]{2,1,0:T(8,128)(2,1)S(1)} %copy-done.5, ...), custom_call_target="tpu_custom_call" | custom-call | tf_op jit(solution)/shard_map/pair_up/pallas_call | solution.py:128
  24.8 1.0 copy-done.9
  25.8 1.0 copy-done.12
  26.8 1.1 collective-permute-start.1
  27.9 2.2 %collective-permute-start.2 = (bf16[2,2,1024,128]{3,2,1,0:T(8,128)(2,1)}, bf16[2,2,1024,128]{3,2,1,0:T(8,128)(2,1)}, u32[]{:S(2)}, u32[]{:S(2)}) collective-permute-start(bf16[2,2,1024,128]{3,2,1,0:T(8,128)(2,1)} %get-tuple-element.44), channel_id=1, source_target_pairs={{0,12},{1,13},{2,14},{3,15},{4,0},{5,1},{6,2},{7,3},{8,4},{9,5},{1... | collective-permute-start | bytes 3145736 | tf_op jit(solution)/shard_map/ppermute | solution.py:549
  30.1 15.2 %all-to-all-done = bf16[128,8,768]{2,1,0:T(8,128)(2,1)S(1)} async-done(((bf16[128,8,768]{2,1,0:T(8,128)(2,1)}), bf16[128,8,768]{2,1,0:T(8,128)(2,1)S(1)}, u32[]{:S(2)}, u32[]{:S(2)}) %all-to-all-start) | async-done | bytes 1572896 | tf_op jit(solution)/shard_map/all_to_all | solution.py:523
  45.2 2.4 %gather_rows.1 = (bf16[2,12,256,128]{3,2,1,0:T(8,128)(2,1)S(1)}, s32[8,1024]{1,0:T(8,128)S(1)}) custom-call(bf16[1024,768]{1,0:T(8,128)(2,1)S(1)} %bitcast.22), custom_call_target="tpu_custom_call" | custom-call | tf_op jit(solution)/shard_map/gather_rows/pallas_call | solution.py:290
  47.7 1.4 collective-permute-start.3
  49.0 1.2 copy-done.10
  50.2 5.3 %sums_1.1 = (f32[2,12,256,128]{3,2,1,0:T(8,128)S(1)}, f32[2,256,128]{2,1,0:T(8,128)S(1)}) custom-call(bf16[2,12,256,128]{3,2,1,0:T(8,128)(2,1)S(1)} %get-tuple-element.39.q_ref, s32[8,1024]{1,0:T(8,128)S(1)} %get-tuple-element.42.place_ref, bf16[2,2,1024,128]{3,2,1,0:T(8,128)(2,1)S(1)} %copy-done.10), custom_call_target="tpu_custom_call" | custom-call | flops 4000000000 | bytes 8388608 | tf_op jit(solution)/shard_map/sums_1/pallas_call | solution.py:366
  55.6 9.1 %sums_2.1 = (f32[2,12,256,128]{3,2,1,0:T(8,128)S(1)}, f32[2,256,128]{2,1,0:T(8,128)S(1)}) custom-call(bf16[2,12,256,128]{3,2,1,0:T(8,128)(2,1)S(1)} %get-tuple-element.39.q_ref, s32[8,1024]{1,0:T(8,128)S(1)} %get-tuple-element.42.place_ref, bf16[2,2,1024,128]{3,2,1,0:T(8,128)(2,1)S(1)} %collective-permute-done.1.refs_0_.refs_2_, ...), custom_call_target="tpu_custom_call" | custom-call | flops 8000000000 | bytes 8388608 | tf_op jit(solution)/shard_map/sums_2/pallas_call | solution.py:366
  64.7 38.0 %finish_prefix.1 = bf16[1024,896]{1,0:T(8,128)(2,1)S(1)} custom-call(bf16[2,12,256,128]{3,2,1,0:T(8,128)(2,1)S(1)} %get-tuple-element.39.q_ref, s32[8,1024]{1,0:T(8,128)S(1)} %get-tuple-element.42.place_ref, f32[2,12,256,128]{3,2,1,0:T(8,128)S(1)} %get-tuple-element.48.sum_ref, f32[2,256,128]{2,1,0:T(8,128)S(1)} %get-tuple-element.49.total_ref, ...), custom_call_target="tpu_custom_call" | custom-call | flops 6000000000 | bytes 8388608 | tf_op jit(solution)/shard_map/finish_prefix/pallas_call | solution.py:460
  102.8 1.2 copy-done
  104.0 36.0 %all-to-all-start.1 = ((bf16[128,8,896]{2,1,0:T(8,128)(2,1)}), bf16[128,8,896]{2,1,0:T(8,128)(2,1)S(1)}, u32[]{:S(2)}, u32[]{:S(2)}) async-start(bf16[128,8,896]{2,1,0:T(8,128)(2,1)} %bitcast.23), calls=%async_computation.1 | async-start | bytes 3670016 | tf_op jit(solution)/shard_map/all_to_all | solution.py:523
  140.1 0.2 convert_reduce_fusion
  140.4 0.1 multiply_add_fusion
  140.5 0.1 reshape.329.at_ref
  140.6 0.2 reshape.325
  140.8 0.8 pad.4.q_ref
  141.5 7.0 %suffix.1 = (f32[8,8,16,128]{3,2,1,0:T(8,128)}, f32[8,8,16,128]{3,2,1,0:T(8,128)}) custom-call(s32[8,16]{1,0:T(8,128)} %table_ref.1, s32[8]{0:T(128)} %len_ref.1, bf16[8,8,16,128]{3,2,1,0:T(8,128)(2,1)} %pad.4.q_ref, bf16[128,16,2048]{2,1,0:T(8,128)(2,1)} %pool_ref.1), custom_call_target="tpu_custom_call" | custom-call | flops 1000000000 | bytes 9437184 | tf_op jit(solution)/shard_map/suffix/pallas_call | solution.py:240
  148.5 1.1 reshape.326.so_ref
  149.6 1.1 reshape.327.sl_ref
  150.7 16.1 %all-to-all-done.1 = bf16[128,8,896]{2,1,0:T(8,128)(2,1)S(1)} async-done(((bf16[128,8,896]{2,1,0:T(8,128)(2,1)}), bf16[128,8,896]{2,1,0:T(8,128)(2,1)S(1)}, u32[]{:S(2)}, u32[]{:S(2)}) %all-to-all-start.1) | async-done | bytes 1835040 | tf_op jit(solution)/shard_map/all_to_all | solution.py:523
  166.8 2.2 %merge.1 = bf16[8,12288]{1,0:T(8,128)(2,1)} custom-call(s32[256,1]{1,0:T(8,128)S(1)} %reshape.329.at_ref, bf16[1024,896]{1,0:T(8,128)(2,1)S(1)} %bitcast.21, f32[8,12288]{1,0:T(8,128)S(1)} %reshape.326.so_ref, f32[8,12288]{1,0:T(8,128)S(1)} %reshape.327.sl_ref), custom_call_target="tpu_custom_call" | custom-call | tf_op jit(solution)/shard_map/merge/pallas_call | solution.py:513
  (28 shorter events, 0.3 us)
Async XLA Ops:
  0.0 0.9 copy-start.1
  0.9 0.7 copy-start.7
  9.4 11.4 %copy-start.3 = (bf16[2,1024,128]{2,1,0:T(8,128)(2,1)S(1)}, bf16[2,1024,128]{2,1,0:T(8,128)(2,1)}, u32[]{:S(2)}) copy-start(bf16[2,1024,128]{2,1,0:T(8,128)(2,1)} %get-tuple-element.32.refs_0_) | copy-start | bytes 1572868
  9.4 11.4 %copy-start.4 = (bf16[2,1024,128]{2,1,0:T(8,128)(2,1)S(1)}, bf16[2,1024,128]{2,1,0:T(8,128)(2,1)}, u32[]{:S(2)}) copy-start(bf16[2,1024,128]{2,1,0:T(8,128)(2,1)} %get-tuple-element.33.refs_1_) | copy-start | bytes 1572868
  9.4 11.4 %copy-start.5 = (bf16[2,1024,128]{2,1,0:T(8,128)(2,1)S(1)}, bf16[2,1024,128]{2,1,0:T(8,128)(2,1)}, u32[]{:S(2)}) copy-start(bf16[2,1024,128]{2,1,0:T(8,128)(2,1)} %get-tuple-element.34.refs_2_) | copy-start | bytes 1572868
  9.4 11.3 %collective-permute-start = (bf16[4,2,1024,128]{3,2,1,0:T(8,128)(2,1)}, bf16[4,2,1024,128]{3,2,1,0:T(8,128)(2,1)}, u32[]{:S(2)}, u32[]{:S(2)}) collective-permute-start(bf16[4,2,1024,128]{3,2,1,0:T(8,128)(2,1)} %get-tuple-element.36), channel_id=1, source_target_pairs={{0,16},{1,17},{2,18},{3,19},{4,20},{5,21},{6,22},{7,23},{8,24},{9,... | collective-permute-start | bytes 6291464 | tf_op jit(solution)/shard_map/ppermute | solution.py:544
  9.5 35.7 %all-to-all-start = ((bf16[128,8,768]{2,1,0:T(8,128)(2,1)}), bf16[128,8,768]{2,1,0:T(8,128)(2,1)S(1)}, u32[]{:S(2)}, u32[]{:S(2)}) async-start(bf16[128,8,768]{2,1,0:T(8,128)(2,1)} %bitcast.9), calls=%async_computation | async-start | bytes 3145728 | tf_op jit(solution)/shard_map/all_to_all | solution.py:523
  20.8 1.0 copy-start.6
  24.8 1.0 copy-start.9
  25.8 1.0 copy-start.12
  26.8 28.7 %collective-permute-start.1 = (bf16[2,2,1024,128]{3,2,1,0:T(8,128)(2,1)}, bf16[2,2,1024,128]{3,2,1,0:T(8,128)(2,1)S(1)}, u32[]{:S(2)}, u32[]{:S(2)}) collective-permute-start(bf16[2,2,1024,128]{3,2,1,0:T(8,128)(2,1)} %get-tuple-element.43), channel_id=1, source_target_pairs={{0,4},{1,5},{2,6},{3,7},{4,8},{5,9},{6,10},{7,11},{8,12},{9,13},{1... | collective-permute-start | bytes 3145736 | tf_op jit(solution)/shard_map/ppermute | solution.py:548
  27.9 27.7 %collective-permute-start.2 = (bf16[2,2,1024,128]{3,2,1,0:T(8,128)(2,1)}, bf16[2,2,1024,128]{3,2,1,0:T(8,128)(2,1)}, u32[]{:S(2)}, u32[]{:S(2)}) collective-permute-start(bf16[2,2,1024,128]{3,2,1,0:T(8,128)(2,1)} %get-tuple-element.44), channel_id=1, source_target_pairs={{0,12},{1,13},{2,14},{3,15},{4,0},{5,1},{6,2},{7,3},{8,4},{9,5},{1... | collective-permute-start | bytes 3145736 | tf_op jit(solution)/shard_map/ppermute | solution.py:549
  47.7 17.0 %collective-permute-start.3 = (bf16[2,2,1024,128]{3,2,1,0:T(8,128)(2,1)}, bf16[2,2,1024,128]{3,2,1,0:T(8,128)(2,1)S(1)}, u32[]{:S(2)}, u32[]{:S(2)}) collective-permute-start(bf16[2,2,1024,128]{3,2,1,0:T(8,128)(2,1)} %copy-done.12), channel_id=1, source_target_pairs={{0,8},{1,9},{2,10},{3,11},{4,12},{5,13},{6,14},{7,15},{8,0},{9,1},... | collective-permute-start | bytes 3145736 | tf_op jit(solution)/shard_map/ppermute | solution.py:552
  49.0 1.2 copy-start.10
  55.6 9.1 %copy-start.11 = (bf16[2,2,1024,128]{3,2,1,0:T(8,128)(2,1)S(1)}, bf16[2,2,1024,128]{3,2,1,0:T(8,128)(2,1)}, u32[]{:S(2)}) copy-start(bf16[2,2,1024,128]{3,2,1,0:T(8,128)(2,1)} %copy-done.9) | copy-start | bytes 3145732
  102.8 1.3 copy-start
  104.0 36.0 %copy-start.8 = (s32[8,1]{0,1:T(1,128)S(1)}, s32[8,1]{0,1:T(1,128)}, u32[]{:S(2)}) copy-start(s32[8,1]{0,1:T(1,128)} %param.7) | copy-start | bytes 100
  104.0 36.6 %copy-start.2 = (bf16[8,12288]{1,0:T(8,128)(2,1)S(1)}, bf16[8,12288]{1,0:T(8,128)(2,1)}, u32[]{:S(2)}) copy-start(bf16[8,12288]{1,0:T(8,128)(2,1)} %q_ref.1) | copy-start | bytes 589828
  104.0 62.8 %all-to-all-start.1 = ((bf16[128,8,896]{2,1,0:T(8,128)(2,1)}), bf16[128,8,896]{2,1,0:T(8,128)(2,1)S(1)}, u32[]{:S(2)}, u32[]{:S(2)}) async-start(bf16[128,8,896]{2,1,0:T(8,128)(2,1)} %bitcast.23), calls=%async_computation.1 | async-start | bytes 3670016 | tf_op jit(solution)/shard_map/all_to_all | solution.py:523
